TPU v7x, 32 devices: a whole 2x2x4 slice. The times are simulated.
32 devices in a mesh: seq: 8 (over z, x), rep: 4 (over y, core).
Axes of the slice: x: 2, y: 2, z: 4, core: 2. Of those that a mesh axis runs over, the one named last changes fastest.
Arguments:
- tokens: bfloat16 [4, 2048, 768], P('rep', 'seq'), may hold values from -6 to 6
- segments: int32 [4, 2048], P('rep', 'seq'), may hold values from 0 to 7, never falling along the last dimension, each value on 1 to 512 neighbouring positions
- orders: int32 [4, 12, 2048], P('rep'), may hold values from 0 to 2047, as said below
- owners: int32 [4, 12, 16], P('rep'), may hold values from 0 to 7, as said below
- query_weight: bfloat16 [768, 768], replicated, may hold values from -0.21875 to 0.21875
- query_bias: bfloat16 [768], replicated, may hold values from -3 to 3
- key_weight: bfloat16 [768, 768], replicated, may hold values from -0.21875 to 0.21875
- value_weight: bfloat16 [768, 768], replicated, may hold values from -0.21875 to 0.21875
- value_bias: bfloat16 [768], replicated, may hold values from -3 to 3
- out_weight: bfloat16 [768, 768], replicated, may hold values from -0.875 to 0.875
- out_bias: bfloat16 [768], replicated, may hold values from -3 to 3
- first_gain: bfloat16 [768], replicated, may hold values from 0.5 to 1.5
- first_shift: bfloat16 [768], replicated, may hold values from -3 to 3
- inner_weight: bfloat16 [768, 3072], replicated, may hold values from -0.21875 to 0.21875
- inner_bias: bfloat16 [3072], replicated, may hold values from -3 to 3
- outer_weight: bfloat16 [3072, 768], replicated, may hold values from -0.109375 to 0.109375
- outer_bias: bfloat16 [768], replicated, may hold values from -3 to 3
- second_gain: bfloat16 [768], replicated, may hold values from 0.5 to 1.5
- second_shift: bfloat16 [768], replicated, may hold values from -3 to 3
- cotangent: bfloat16 [4, 2048, 768], P('rep', 'seq'), may hold values from -6 to 6
Outputs:
- output: bfloat16 [4, 2048, 768], P('rep', 'seq')
- gradient_tokens: bfloat16 [4, 2048, 768], P('rep', 'seq')
- gradient_query_weight: float32 [768, 768], P('seq')
- gradient_query_bias: float32 [768], P('seq')
- gradient_key_weight: float32 [768, 768], P('seq')
- gradient_value_weight: float32 [768, 768], P('seq')
- gradient_value_bias: float32 [768], P('seq')
- gradient_out_weight: float32 [768, 768], P('seq')
- gradient_out_bias: float32 [768], P('seq')
- gradient_first_gain: float32 [768], P('seq')
- gradient_first_shift: float32 [768], P('seq')
- gradient_inner_weight: float32 [768, 3072], P('seq')
- gradient_inner_bias: float32 [3072], P('seq')
- gradient_outer_weight: float32 [3072, 768], P('seq')
- gradient_outer_bias: float32 [768], P('seq')
- gradient_second_gain: float32 [768], P('seq')
- gradient_second_shift: float32 [768], P('seq')
- cluster_stats: float32 [2, 12, 8], replicated
Inputs may be any that keep to these rules, and one draw needn't show every extreme that they name: `orders`: for each group and head, a permutation of the group's 2048 positions. For every head, the 256 tokens in the clusters that owners gives to one device hold exactly 32 tokens of each device's block of 256 tokens. `owners`: for each group and head, every device owns exactly 2 of the 16 clusters.
All inputs are finite; a program needn't handle non-finite values.
Results may differ from a plain program's by a relative error of at most 0.015.
Values may be sent and summed in bfloat16 or wider, within the bound.
A program may use at most 192 MiB of HBM per device.

v0:
```python
import functools

import jax
import jax.numpy as jnp
from jax import lax
from jax.experimental import pallas as pl
from jax.experimental.pallas import tpu as pltpu
from jax.sharding import PartitionSpec as P

EPSILON = 1e-12
NEGATIVE = -1e30


def norm_forward(hidden, gain_vector, shift_vector):
    centre = hidden - jnp.mean(hidden, axis=-1, keepdims=True)
    root_inverse = lax.rsqrt(jnp.mean(centre * centre, axis=-1, keepdims=True) + EPSILON)
    normed = centre * root_inverse
    return (
        normed * gain_vector.astype(jnp.float32) + shift_vector.astype(jnp.float32),
        normed,
        root_inverse,
    )


def norm_backward(upstream, normed, root_inverse, gain_vector):
    scaled = upstream * gain_vector.astype(jnp.float32)
    return root_inverse * (
        scaled
        - jnp.mean(scaled, axis=-1, keepdims=True)
        - normed * jnp.mean(scaled * normed, axis=-1, keepdims=True)
    )


def exact_gelu(inner_sum):
    return jax.nn.gelu(inner_sum, approximate=False)


def rank_matrix(sort_keys):
    row_count = sort_keys.shape[1]
    ranks = jnp.sum((sort_keys[:, None, :] < sort_keys[:, :, None]).astype(jnp.int32), axis=2)
    return (ranks[:, None, :] == jnp.arange(row_count, dtype=jnp.int32)[None, :, None]).astype(
        jnp.bfloat16
    )


def scatter_rows(row_block, placing, seq_count):
    head_count, row_count, features = row_block.shape
    picked = jnp.einsum(
        "hri,hif->hrf", placing, row_block, preferred_element_type=jnp.float32
    ).astype(jnp.bfloat16)
    return picked.reshape(head_count, seq_count, row_count // seq_count * features).transpose(
        1, 0, 2
    )


def collect_rows(packed, placing, features):
    seq_count, head_count, flat_width = packed.shape
    row_block = packed.transpose(1, 0, 2).reshape(
        head_count, seq_count * flat_width // features, features
    )
    return jnp.einsum(
        "hri,hrf->hif", placing, row_block, preferred_element_type=jnp.float32
    ).astype(jnp.bfloat16)


def cluster_scores(queries, keys_in, segment_ids, score_scale):
    scores = (
        jnp.einsum("nqd,nkd->nqk", queries, keys_in, preferred_element_type=jnp.float32)
        * score_scale
    )
    allowed = segment_ids[:, :, None] == segment_ids[:, None, :]
    return (scores, allowed, jnp.where(allowed, scores, NEGATIVE))


def cluster_forward(queries, keys_in, values, segment_ids, score_scale):
    scores, allowed, masked = cluster_scores(queries, keys_in, segment_ids, score_scale)
    highest = jnp.max(masked, axis=-1, keepdims=True)
    raised = jnp.exp(masked - highest)
    totals = jnp.sum(raised, axis=-1, keepdims=True)
    weights = raised / totals
    attended = jnp.einsum(
        "nqk,nkd->nqd", weights.astype(jnp.bfloat16), values, preferred_element_type=jnp.float32
    ).astype(jnp.bfloat16)
    log_total = highest[:, :, 0] + jnp.log(totals[:, :, 0])
    entropy = log_total - jnp.sum(weights * jnp.where(allowed, scores, 0.0), axis=-1)
    occupied = jnp.sum(allowed.astype(jnp.float32), axis=-1)
    return (attended, log_total, entropy, occupied)


def cluster_backward(queries, keys_in, values, segment_ids, log_total, grad_out, score_scale):
    masked = cluster_scores(queries, keys_in, segment_ids, score_scale)[2]
    weights = jnp.exp(masked - log_total[:, :, None])
    weight_grads = jnp.einsum("nqd,nkd->nqk", grad_out, values, preferred_element_type=jnp.float32)
    value_grads = jnp.einsum(
        "nqk,nqd->nkd", weights.astype(jnp.bfloat16), grad_out, preferred_element_type=jnp.float32
    )
    score_grads = (
        weights * (weight_grads - jnp.sum(weights * weight_grads, axis=-1, keepdims=True))
    ).astype(jnp.bfloat16)
    query_grads = (
        jnp.einsum("nqk,nkd->nqd", score_grads, keys_in, preferred_element_type=jnp.float32)
        * score_scale
    )
    key_grads = (
        jnp.einsum("nqk,nqd->nkd", score_grads, queries, preferred_element_type=jnp.float32)
        * score_scale
    )
    return jnp.stack([query_grads, key_grads, value_grads], axis=2).astype(jnp.bfloat16)


MESH = pl.DeviceIdType.MESH


UNROLL = 8
PIECES = 4
FIRST = 1


def half_roll(block):
    return jnp.concatenate([block[:, 64:], block[:, :64]], axis=1)


def lanes(shape):
    return lax.broadcasted_iota(jnp.int32, shape, len(shape) - 1)


def bits(value, flip):
    return value + flip - 2 * value * flip


def coordinates():
    s, r = lax.axis_index("seq"), lax.axis_index("rep")
    return s // 4, (s // 2) % 2, s % 2, r // 2, r % 2


def device(zh, zl, x, y, c):
    return (4 * zh + 2 * zl + x, 2 * y + c)


def greet(peers):
    barrier = pltpu.get_barrier_semaphore()
    for peer in peers:
        pl.semaphore_signal(barrier, inc=1, device_id=peer, device_id_type=MESH)
    pl.semaphore_wait(barrier, len(peers))


def remote(src, dst, sems, index, peer):
    return pltpu.make_async_remote_copy(
        src_ref=src,
        dst_ref=dst,
        send_sem=sems[0].at[index],
        recv_sem=sems[1].at[index],
        device_id=peer,
        device_id_type=MESH,
    )


def dot(left, right, left_dim=1, right_dim=0):
    return lax.dot_general(
        left,
        right,
        (((left_dim,), (right_dim,)), ((), ())),
        preferred_element_type=jnp.float32,
    )


def hot(condition):
    return jnp.where(condition, 1.0, 0.0).astype(jnp.bfloat16)


def build_gather(order_ref, row, start, count, into):
    tokens = into.shape[1]

    def one(k, carry):
        at = pl.multiple_of(k * 128, 128)
        ids = order_ref[row : row + 1, pl.ds(pl.multiple_of(start + at, 128), 128)]
        column = jnp.broadcast_to(ids.astype(jnp.float32), (128, 128)).T
        lane = lanes((128, 128)).astype(jnp.float32)
        for t in range(tokens // 128):
            into[pl.ds(at, 128), t * 128 : (t + 1) * 128] = hot(column == lane + 128.0 * t)
        return carry

    lax.fori_loop(0, count // 128, one, 0)


def build_scatter(order_ref, half, first_token, into):
    group = order_ref.shape[1]

    def one(k, carry):
        at = pl.multiple_of(k * 128, 128)
        token = lax.broadcasted_iota(jnp.int32, (128, 128), 0) + (first_token + at)
        for p in range(into.shape[1] // 128):
            row, start = (0, 128 * p) if 128 * p < group else (1, half + 128 * p - group)
            ids = order_ref[row : row + 1, pl.ds(pl.multiple_of(start, 128), 128)]
            into[pl.ds(at, 128), 128 * p : 128 * (p + 1)] = hot(ids == token)
        return carry

    lax.fori_loop(0, into.shape[0] // 128, one, 0)


def select_head(slab, half, place):
    return jnp.where(half == place, slab, half_roll(slab))


def join(low_lanes, high_lanes):
    return jnp.where(lanes(low_lanes.shape) < 64, low_lanes, high_lanes)


def pick_columns(pairs, j, c):
    (q_one, q_two), (k_one, k_two), (v_one, v_two) = pairs
    zero = jnp.zeros_like(q_one)
    q1, v1, k1 = select_head(q_one, c, 0), select_head(v_one, c, 1), select_head(k_one, c, 0)
    v2, q2, k2 = (
        select_head(v_two, j % 2, 0),
        select_head(q_two, j % 2, 1),
        select_head(k_two, j % 2, 1),
    )
    return join(q1, v1), join(k1, zero), join(v2, q2), join(zero, k2)


def normalize(hidden):
    centre = hidden - jnp.mean(hidden, axis=1, keepdims=True)
    root_inverse = lax.rsqrt(jnp.mean(centre * centre, axis=1, keepdims=True) + EPSILON)
    return centre * root_inverse, root_inverse


def normalize_back(scaled, normed, root_inverse):
    return root_inverse * (
        scaled
        - jnp.mean(scaled, axis=1, keepdims=True)
        - normed * jnp.mean(scaled * normed, axis=1, keepdims=True)
    )


def forward_kernel(
    tokens_ref,
    cot_ref,
    seg_ref,
    orders_ref,
    owners_ref,
    query_bias_ref,
    value_bias_ref,
    out_bias_ref,
    first_gain_ref,
    first_shift_ref,
    outer_bias_ref,
    second_gain_ref,
    second_shift_ref,
    inner_bias_ref,
    wq_hbm,
    wk_hbm,
    wv_hbm,
    out_w_hbm,
    inner_w_hbm,
    outer_w_hbm,
    wsel_hbm,
    order_hbm,
    stats_hbm,
    x_hbm,
    sorted_hbm,
    prob_hbm,
    att_hbm,
    low_hbm,
    act_hbm,
    output_hbm,
    dsecond_hbm,
    dinner_hbm,
    delta_hbm,
    dbranch_hbm,
    vec_hbm,
    datt_hbm,
    wsel_ref,
    order_ref,
    stats_ref,
    x_all,
    sorted_ref,
    prob_ref,
    att_ref,
    low_ref,
    act_ref,
    output_ref,
    dsecond_ref,
    dinner_ref,
    delta_ref,
    dbranch_ref,
    vec_out,
    datt_ref,
    cot_my,
    weights,
    orders_in,
    owners_in,
    owner_pad,
    seg_src,
    seg_all,
    bias_rows,
    bias_sel,
    tok,
    gather,
    scatter,
    att_sorted,
    att_send,
    att_in,
    ent_ref,
    cnt_ref,
    swap_send,
    swap_recv,
    ring_send,
    ring_recv,
    seg_send,
    seg_recv,
    back_send,
    back_recv,
    local_sem,
    out_w,
    inner_w,
    outer_w,
    slope,
    total,
    normed_ref,
    bias_ref,
    load_sem,
    store_sem,
):
    zh, zl, x, y, c = coordinates()
    j = 2 * zl + x
    p = 4 * c + j
    block, width = tokens_ref.shape
    group = 8 * block
    scale = 0.125
    swap = (swap_send, swap_recv)
    ring = (ring_send, ring_recv)
    seg_sems = (seg_send, seg_recv)
    back = (back_send, back_recv)

    def member(flip):
        fc, fz, fx = flip // 4, (flip // 2) % 2, flip % 2
        mc, mz, mx = bits(c, fc), bits(zl, fz), bits(x, fx)
        return device(zh, mz, mx, y, mc), 4 * mc + 2 * mz + mx

    swap_peer = device(1 - zh, zl, x, y, 1 - c)
    peers = [member(flip)[0] for flip in range(1, 8)]
    sibling = peers[3]
    over_x, over_z = peers[0], peers[1]
    matched = c == zh

    slabs = [
        pltpu.make_async_copy(
            src.at[:, pl.ds(pl.multiple_of(index * 128, 128), 128)],
            weights.at[i, slot],
            local_sem.at[3 * slot + i],
        )
        for i, src in enumerate((wq_hbm, wk_hbm, wv_hbm))
        for slot, index in enumerate((j, 4 + j // 2))
    ]
    for copy in slabs:
        copy.start()
    greet(peers + [swap_peer])
    width_inner = inner_w.shape[1]
    dense_tile = 2 * width
    parts = [slice(dense_tile * t, dense_tile * (t + 1)) for t in range(width_inner // dense_tile)]
    loads = [pltpu.make_async_copy(out_w_hbm, out_w, load_sem.at[0])]
    for t, at in enumerate(parts):
        loads.append(
            pltpu.make_async_copy(inner_w_hbm.at[:, at], inner_w.at[:, at], load_sem.at[1 + 2 * t])
        )
        loads.append(pltpu.make_async_copy(outer_w_hbm.at[at], outer_w.at[at], load_sem.at[2 + 2 * t]))
    kept = {
        "wsel": (wsel_ref, wsel_hbm),
        "order": (order_ref, order_hbm),
        "stats": (stats_ref, stats_hbm),
        "x": (x_all, x_hbm),
        "sorted": (sorted_ref, sorted_hbm),
        "prob": (prob_ref, prob_hbm),
        "att": (att_ref, att_hbm),
        "low": (low_ref, low_hbm),
        "act": (act_ref, act_hbm),
        "output": (output_ref, output_hbm),
        "dsecond": (dsecond_ref, dsecond_hbm),
        "dinner": (dinner_ref, dinner_hbm),
        "delta": (delta_ref, delta_hbm),
        "dbranch": (dbranch_ref, dbranch_hbm),
        "vec": (vec_out, vec_hbm),
        "datt": (datt_ref, datt_hbm),
    }
    stores = {
        name: pltpu.make_async_copy(src, dst, store_sem.at[i]) for i, (name, (src, dst)) in enumerate(kept.items())
    }

    seg_src[...] = jnp.broadcast_to(seg_ref[...], seg_src.shape)
    table_copies = [
        remote(orders_ref, orders_in, swap, 0, sibling),
        remote(owners_ref, owners_in, swap, 1, sibling),
    ]
    for copy in table_copies:
        copy.start()
    p_swap = 4 * (1 - c) + j
    chunks = PIECES
    halves = [pl.ds(i * (block // chunks), block // chunks) for i in range(chunks)]
    pairs = [(tokens_ref.at[at], x_all.at[p_swap, at], x_all.at[p, at]) for at in halves]
    pairs.insert(0, (seg_src, seg_all.at[p_swap], seg_all.at[p]))
    pairs.append((cot_ref, cot_my, cot_my))
    swaps = [remote(src, dst, swap, 2 + i, swap_peer) for i, (src, dst, _) in enumerate(pairs)]
    locals_ = [
        pltpu.make_async_copy(src, own, swap_recv.at[4 + chunks + i]) for i, (src, _, own) in enumerate(pairs)
    ]

    px, pz, pd = member(1)[1], member(2)[1], member(3)[1]

    def share_block(index, position, i, peer):
        view = x_all.at[position, halves[i]]
        return remote(view, view, ring, index, peer)

    every = range(chunks)
    own_to_x = [share_block(i, p, i, over_x) for i in every]
    own_to_z = [share_block(chunks + i, p, i, over_z) for i in every]
    own_to_s = [share_block(2 * chunks + i, p, i, sibling) for i in every]
    x_to_s = [share_block(3 * chunks + i, px, i, sibling) for i in every]
    z_to_s = [share_block(4 * chunks + i, pz, i, sibling) for i in every]
    d_to_s = [share_block(5 * chunks + i, pd, i, sibling) for i in every]
    relays = [
        share_block(6 * chunks + i, px, i, over_z) if i < FIRST else share_block(6 * chunks + i, pz, i, over_x)
        for i in every
    ]
    seg_copies = [
        remote(seg_all.at[p], seg_all.at[p], seg_sems, flip - 1, peers[flip - 1]) for flip in range(1, 8)
    ]
    opposite = jnp.logical_not(matched)

    def own_half(i, arrivals):
        arrivals[1 + i].wait()
        own_to_x[i].start()
        own_to_z[i].start()
        own_to_s[i].start()

    def segments_out(arrivals):
        arrivals[0].wait()
        for copy in seg_copies:
            copy.start()

    def relay(i):
        own_to_x[i].wait()
        own_to_z[i].wait()
        relays[i].start()
        x_to_s[i].start()
        z_to_s[i].start()

    def relay_end(i):
        relays[i].wait()
        d_to_s[i].start()

    def wait_sibling():
        for copy in own_to_s + x_to_s + z_to_s + d_to_s:
            copy.wait_recv()

    @pl.when(matched)
    def _():
        for copy in locals_:
            copy.start()
        segments_out(locals_)
        for i in every:
            own_half(i, locals_)

    @pl.when(opposite)
    def _():
        for copy in swaps[: 1 + chunks]:
            copy.start()

    for copy in slabs:
        copy.wait()
    tiles = pick_columns([[weights[i, slot].astype(jnp.float32) for slot in range(2)] for i in range(3)], j, c)
    for i, tile in enumerate(tiles):
        wsel_ref[:, 128 * i : 128 * (i + 1)] = tile.astype(jnp.bfloat16)
    for i, ref in enumerate((query_bias_ref, None, value_bias_ref)):
        row = jnp.zeros((1, width), jnp.float32) if ref is None else ref[...].astype(jnp.float32).reshape(1, width)
        bias_rows[i : i + 1, :] = row
    bias_pairs = [
        [bias_rows[i : i + 1, pl.ds(pl.multiple_of(index * 128, 128), 128)] for index in (j, 4 + j // 2)]
        for i in range(3)
    ]
    for i, tile in enumerate(pick_columns(bias_pairs, j, c)):
        bias_sel[0:1, 128 * i : 128 * (i + 1)] = tile

    for copy in table_copies:
        copy.wait()
    h1, h2 = 2 * j + c, 8 + j
    for i, h in enumerate((h1, h2)):
        order_ref[i : i + 1, :] = jnp.where(matched, orders_ref[h], orders_in[h])
    half = 1024 * c

    build_gather(order_ref, 0, 0, group, gather.at[pl.ds(0, group)])

    @pl.when(matched)
    def _():
        for i in every:
            relay(i)

    @pl.when(opposite)
    def _():
        segments_out(swaps)
        for i in range(chunks // 2):
            own_half(i, swaps)

    build_gather(order_ref, 1, half, group // 2, gather.at[pl.ds(group, group // 2)])

    @pl.when(matched)
    def _():
        for i in every:
            relay_end(i)

    @pl.when(opposite)
    def _():
        for i in range(chunks // 2, chunks):
            own_half(i, swaps)
        for i in range(chunks // 2):
            relay(i)

    def project(position):
        at = pl.ds(pl.multiple_of(position * block, block), block)
        out = dot(x_all[position], wsel_ref[...]) + bias_sel[0:1, :]
        ids = seg_all[position, 0:1, :].astype(jnp.float32)
        columns = [
            jnp.broadcast_to(ids[:, 128 * i : 128 * (i + 1)], (128, 128)).T for i in range(block // 128)
        ]
        lane = lanes((block, 128))
        seg_hot = hot(jnp.concatenate(columns, axis=0) == (lane % 64).astype(jnp.float32))
        low = out.astype(jnp.bfloat16)
        tok[at, 0:128] = low[:, 0:128]
        tok[at, 128:256] = jnp.where(lane < 64, low[:, 128:256], seg_hot)
        tok[at, 256:384] = low[:, 256:384]
        tok[at, 384:512] = jnp.where(lane < 64, seg_hot, low[:, 384:512])

    step = 512
    early, late = group // 2 * zh, group // 2 * (1 - zh)

    def gather_rows(start, add):
        tokens = pl.ds(pl.multiple_of(start, group // 2), group // 2)

        def one(first, columns):
            def body(k, carry):
                at = pl.ds(pl.multiple_of(k * step, step), step)
                rows = dot(gather[at, tokens], tok[tokens, columns])
                if add:
                    sorted_ref[at, :] = (rows + sorted_ref[at, :].astype(jnp.float32)).astype(jnp.bfloat16)
                else:
                    sorted_ref[at, :] = rows.astype(jnp.bfloat16)
                return carry

            return body

        lax.fori_loop(0, group // step, one(0, pl.ds(0, 256)), 0)
        lax.fori_loop(group // step, group * 3 // 2 // step, one(1, pl.ds(256, 256)), 0)

    for copy in seg_copies:
        copy.wait()
    pl.when(opposite)(wait_sibling)
    for k in range(4):
        project(4 * zh + k)

    @pl.when(opposite)
    def _():
        for i in range(chunks // 2, chunks):
            relay(i)
        for i in range(chunks // 2):
            relay_end(i)

    gather_rows(early, False)

    @pl.when(opposite)
    def _():
        for i in range(chunks // 2, chunks):
            relay_end(i)

    def build_block(i, carry):
        build_scatter(order_ref, half, member(7 - i)[1] * block, scatter.at[i % 4])
        return carry

    lax.fori_loop(0, 4, build_block, 0)
    pl.when(matched)(wait_sibling)
    for k in range(4):
        project(4 * (1 - zh) + k)
    for name in ("x", "wsel", "order"):
        stores[name].start()
    for copy in loads:
        copy.start()


    @pl.when(opposite)
    def _():
        swaps[1 + chunks].start()

    gather_rows(late, True)
    def attend(first_lanes):
        def one(i, carry):
            at = pl.ds(pl.multiple_of(i * 128, 128), 128)
            tile_zero, tile_one = sorted_ref[at, 0:128], sorted_ref[at, 128:256]
            low_lanes = lanes((128, 128)) < 64
            query_lanes = low_lanes if first_lanes else jnp.logical_not(low_lanes)
            queries = jnp.where(query_lanes, tile_zero, jnp.zeros_like(tile_zero))
            ids = jnp.where(query_lanes, jnp.zeros_like(tile_one), tile_one)
            both = dot(jnp.concatenate([queries, ids], axis=0), tile_one, 1, 1)
            scores, allowed = both[:128] * scale, both[128:]
            masked = jnp.where(allowed > 0.5, scores, NEGATIVE)
            highest = jnp.max(masked, axis=1, keepdims=True)
            raised = jnp.exp(masked - highest)
            totals = jnp.sum(raised, axis=1, keepdims=True)
            weights = raised * (1.0 / totals)
            prob_ref[at, :] = weights
            mixed = dot(weights.astype(jnp.bfloat16), tile_zero)
            att_sorted[at, :] = jnp.where(query_lanes, 0.0, mixed).astype(jnp.bfloat16)
            log_total = highest + jnp.log(totals)
            entropy = jnp.where(lanes((128, 128)) == 0, log_total, 0.0) - weights * masked
            ent_ref[pl.ds(i, 1), :] = jnp.sum(entropy, axis=0, keepdims=True)
            cnt_ref[pl.ds(i, 1), :] = jnp.sum(allowed, axis=0, keepdims=True)
            return carry

        return one

    lax.fori_loop(0, 16, attend(True), 0, unroll=UNROLL)
    lax.fori_loop(16, 24, attend(False), 0, unroll=UNROLL)
    stores["sorted"].start()
    stores["prob"].start()

    def send_back(i, carry):
        flip = 7 - i
        peer = member(flip)[0]
        att_send[flip] = dot(scatter[i % 4], att_sorted[...]).astype(jnp.bfloat16)

        @pl.when(i < 7)
        def _():
            remote(att_send.at[flip], att_in.at[p], back, flip, peer).start()

        @pl.when(i < 4)
        def _():
            build_block(i + 4, 0)

        return carry

    lax.fori_loop(0, 8, send_back, 0)
    back_copies = [remote(att_send.at[flip], att_in.at[p], back, flip, peers[flip - 1]) for flip in range(1, 8)]
    att_in[p] = att_send[0]

    stats_ref[...] = jnp.zeros_like(stats_ref)
    owner_pad[...] = jnp.full_like(owner_pad, -1.0)
    clusters = owners_ref.shape[2]
    for h, first, size, skip in ((h1, 0, clusters, 0), (h2, clusters, clusters // 2, c)):
        ids = jnp.where(matched, owners_ref[h], owners_in[h])
        owner_pad[0:1, 0:clusters] = ids.astype(jnp.float32)
        column = jnp.broadcast_to(owner_pad[0:1, :], (128, 128)).T
        column = jnp.where(skip == 1, column[clusters // 2 : clusters // 2 + size], column[0:size])
        owned = jnp.where(column == lanes((size, 128)).astype(jnp.float32), 1.0, 0.0)
        for kind, (lane_sums, divisor) in enumerate(((ent_ref, 4.0 * block), (cnt_ref, 4.0 * block * 128))):
            sums = jnp.sum(lane_sums[first : first + size, :], axis=1, keepdims=True) / divisor
            stats_ref[kind, pl.ds(h, 1), :] = jnp.sum(sums * owned, axis=0, keepdims=True)

    stores["stats"].start()
    bias_ref[0:1, :] = inner_bias_ref[...].astype(jnp.float32).reshape(1, width_inner)
    out_bias, first_gain, first_shift, outer_bias, second_gain, second_shift = (
        ref[...].astype(jnp.float32).reshape(1, width)
        for ref in (
            out_bias_ref,
            first_gain_ref,
            first_shift_ref,
            outer_bias_ref,
            second_gain_ref,
            second_shift_ref,
        )
    )
    for copy in back_copies:
        copy.wait()
    for pair in range(4):
        even, odd = att_in[pair], att_in[4 + pair]
        att_ref[:, 128 * pair : 128 * (pair + 1)] = join(half_roll(even), odd)
    for pair in range(2):
        low_half = att_in[2 * pair] + att_in[4 + 2 * pair]
        high_half = att_in[2 * pair + 1] + att_in[5 + 2 * pair]
        att_ref[:, 512 + 128 * pair : 640 + 128 * pair] = join(low_half, half_roll(high_half))
    stores["att"].start()

    loads[0].wait()
    branch = dot(att_ref[...], out_w[...]) + out_bias
    normed, root_one = normalize(x_all[p].astype(jnp.float32) + branch)
    first = normed * first_gain + first_shift
    normed_ref[...] = normed
    low_ref[...] = first.astype(jnp.bfloat16)
    stores["low"].start()
    total[...] = first + outer_bias
    for copy in loads[1:]:
        copy.wait()

    def dense_forward(t, carry):
        at = pl.ds(pl.multiple_of(t * dense_tile, dense_tile), dense_tile)
        inner = dot(low_ref[...], inner_w[:, at]) + bias_ref[0:1, at]
        cumulative = 0.5 + 0.5 * lax.erf(inner * (0.5**0.5))
        density = jnp.exp(-0.5 * inner * inner) * 0.3989422804014327
        slope[:, at] = cumulative + inner * density
        act = (inner * cumulative).astype(jnp.bfloat16)
        act_ref[:, at] = act
        total[...] += dot(act, outer_w[at, :])
        return carry

    lax.fori_loop(0, len(parts), dense_forward, 0)
    stores["act"].start()

    @pl.when(matched)
    def _():
        locals_[1 + chunks].wait()

    @pl.when(opposite)
    def _():
        swaps[1 + chunks].wait()

    normed_two, root_two = normalize(total[...])
    output_ref[...] = (normed_two * second_gain + second_shift).astype(jnp.bfloat16)
    stores["output"].start()
    upstream = cot_my[...].astype(jnp.float32)
    vec_out[4:5, :] = jnp.sum(upstream * normed_two, axis=0, keepdims=True)
    vec_out[5:6, :] = jnp.sum(upstream, axis=0, keepdims=True)
    delta_two = normalize_back(upstream * second_gain, normed_two, root_two)
    low_two = delta_two.astype(jnp.bfloat16)
    dsecond_ref[...] = low_two
    stores["dsecond"].start()
    vec_out[3:4, :] = jnp.sum(low_two.astype(jnp.float32), axis=0, keepdims=True)
    total[...] = delta_two

    def dense_back(t, carry):
        at = pl.ds(pl.multiple_of(t * dense_tile, dense_tile), dense_tile)
        dact = dot(dsecond_ref[...], outer_w[at, :], 1, 1)
        dinner = (dact * slope[:, at]).astype(jnp.bfloat16)
        dinner_ref[:, at] = dinner
        bias_ref[0:1, at] = jnp.sum(dinner.astype(jnp.float32), axis=0, keepdims=True)
        total[...] += dot(dinner, inner_w[:, at], 1, 1)
        return carry

    lax.fori_loop(0, len(parts), dense_back, 0)
    stores["dinner"].start()
    for i in range(width_inner // width):
        vec_out[6 + i : 7 + i, :] = bias_ref[0:1, width * i : width * (i + 1)]
    delta_first = total[...]
    normed = normed_ref[...]
    vec_out[1:2, :] = jnp.sum(delta_first * normed, axis=0, keepdims=True)
    vec_out[2:3, :] = jnp.sum(delta_first, axis=0, keepdims=True)
    delta_one = normalize_back(delta_first * first_gain, normed, root_one)
    delta_ref[...] = delta_one
    stores["delta"].start()
    low_one = delta_one.astype(jnp.bfloat16)
    dbranch_ref[...] = low_one
    stores["dbranch"].start()
    vec_out[0:1, :] = jnp.sum(low_one.astype(jnp.float32), axis=0, keepdims=True)
    vec_out[10:16, :] = jnp.zeros((6, width), jnp.float32)
    stores["vec"].start()
    datt_ref[...] = dot(dbranch_ref[...], out_w[...], 1, 1).astype(jnp.bfloat16)
    stores["datt"].start()
    for copy in stores.values():
        copy.wait()
    for copy in own_to_s + x_to_s + z_to_s + d_to_s:
        copy.wait_send()


def forward_layer(tokens, cotangent, segments, orders, owners, vectors, weights):
    block, width = tokens.shape
    inner_width = weights[4].shape[1]
    group = 8 * block
    low, full = jnp.bfloat16, jnp.float32
    vmem = pl.BlockSpec(memory_space=pltpu.VMEM)
    hbm = pl.BlockSpec(memory_space=pl.ANY)
    dma = pltpu.SemaphoreType.DMA
    rows = group * 3 // 2
    kept = [
        ((width, 512), low),
        ((8, group), jnp.int32),
        ((2, 16, 128), full),
        ((8, block, width), low),
        ((rows, 256), low),
        ((rows, 128), full),
        ((block, width), low),
        ((block, width), low),
        ((block, inner_width), low),
        ((block, width), low),
        ((block, width), low),
        ((block, inner_width), low),
        ((block, width), full),
        ((block, width), low),
        ((16, width), full),
        ((block, width), low),
    ]
    return pl.pallas_call(
        forward_kernel,
        out_shape=[jax.ShapeDtypeStruct(*one) for one in kept],
        in_specs=[vmem] * 14 + [hbm] * 6,
        out_specs=[hbm] * len(kept),
        scratch_shapes=[pltpu.VMEM(*one) for one in kept]
        + [
            pltpu.VMEM((block, width), low),
            pltpu.VMEM((3, 2, width, 128), low),
            pltpu.VMEM(orders.shape, jnp.int32),
            pltpu.VMEM(owners.shape, jnp.int32),
            pltpu.VMEM((8, 128), full),
            pltpu.VMEM((8, block), jnp.int32),
            pltpu.VMEM((8, 8, block), jnp.int32),
            pltpu.VMEM((8, width), full),
            pltpu.VMEM((8, 512), full),
            pltpu.VMEM((group, 512), low),
            pltpu.VMEM((rows, group), low),
            pltpu.VMEM((4, block, rows), low),
            pltpu.VMEM((rows, 128), low),
            pltpu.VMEM((8, block, 128), low),
            pltpu.VMEM((8, block, 128), low),
            pltpu.VMEM((24, 128), full),
            pltpu.VMEM((24, 128), full),
            dma((2 * PIECES + 6,)),
            dma((2 * PIECES + 6,)),
            dma((7 * PIECES,)),
            dma((7 * PIECES,)),
            dma((7,)),
            dma((7,)),
            dma((8,)),
            dma((8,)),
            dma((6,)),
            pltpu.VMEM(weights[3].shape, low),
            pltpu.VMEM(weights[4].shape, low),
            pltpu.VMEM(weights[5].shape, low),
            pltpu.VMEM((block, inner_width), full),
            pltpu.VMEM((block, width), full),
            pltpu.VMEM((block, width), full),
            pltpu.VMEM((8, inner_width), full),
            dma((1 + inner_width // width,)),
            dma((len(kept),)),
        ],
        compiler_params=pltpu.CompilerParams(
            collective_id=1, has_side_effects=True, vmem_limit_bytes=62 << 20
        ),
        name="forward_layer",
    )(tokens, cotangent, segments, orders, owners, *vectors, *weights)


def rows_of(start, q, size):
    return pl.ds(pl.multiple_of(start * q, 16), size * q)


def add_into(count, target, other):
    def one(i, carry):
        target(i)[...] = (
            target(i)[...].astype(jnp.float32) + other(i)[...].astype(jnp.float32)
        ).astype(jnp.bfloat16)
        return carry

    lax.fori_loop(0, count, one, 0)


def reduce_steps(parts, g_ref, f_ref, buffers, sems):
    core_in, a_one, a_two, a_three, a_four, b_one, b_two, b_three, b_four = buffers
    zh, zl, x, y, c = coordinates()
    q = g_ref.shape[3] // 8
    width = g_ref.shape[4] // parts
    over_c, over_y = device(zh, zl, x, y, 1 - c), device(zh, zl, x, 1 - y, c)
    over_x, over_zl = device(zh, zl, 1 - x, y, c), device(zh, 1 - zl, x, y, c)
    over_zh = device(1 - zh, zl, x, y, c)
    flying = {}

    def send(name, k, src, dst, peer):
        copy = remote(src, dst, (sems[0].at[name], sems[1].at[name]), k, peer)
        copy.start()
        flying[name, k] = copy

    def arrive(name, k):
        flying.pop((name, k)).wait()

    def step(stage, k):
        cols = pl.ds(k * width, width)
        if stage == "0":
            send(
                0, k, g_ref.at[:, :, :, rows_of(4 * (1 - c), q, 4), cols], core_in.at[:, :, :, :, cols], over_c
            )
        if stage == "1":
            arrive(0, k)
            add_into(
                8,
                lambda i: core_in.at[i // 4, (i // 2) % 2, i % 2, :, cols],
                lambda i: g_ref.at[i // 4, (i // 2) % 2, i % 2, rows_of(4 * c, q, 4), cols],
            )
            send(1, k, core_in.at[:, :, 1 - x, pl.ds(0, 2 * q), cols], a_one.at[:, :, :, cols], over_x)
            send(2, k, core_in.at[:, :, :, rows_of(3 - y, q, 1), cols], b_one.at[:, :, :, :, cols], over_y)
        if stage == "2a":
            arrive(1, k)
            add_into(
                4,
                lambda i: a_one.at[i // 2, i % 2, :, cols],
                lambda i: core_in.at[i // 2, i % 2, x, pl.ds(0, 2 * q), cols],
            )
            send(3, k, a_one.at[:, 1 - zl, :, cols], a_two.at[:, :, cols], over_zl)
        if stage == "3a":
            arrive(3, k)
            add_into(2, lambda i: a_two.at[i, :, cols], lambda i: a_one.at[i, zl, :, cols])
            send(4, k, a_two.at[1 - zh, :, cols], a_three.at[:, cols], over_zh)
        if stage == "4a":
            arrive(4, k)
            add_into(1, lambda i: a_three.at[:, cols], lambda i: a_two.at[zh, :, cols])
            send(5, k, a_three.at[:, cols], a_four.at[:, cols], over_y)
        if stage == "2b":
            arrive(2, k)
            add_into(
                8,
                lambda i: b_one.at[i // 4, (i // 2) % 2, i % 2, :, cols],
                lambda i: core_in.at[i // 4, (i // 2) % 2, i % 2, rows_of(2 + y, q, 1), cols],
            )
            send(6, k, b_one.at[:, :, 1 - x, :, cols], b_two.at[:, :, :, cols], over_x)
        if stage == "3":
            arrive(6, k)
            add_into(
                4,
                lambda i: b_two.at[i // 2, i % 2, :, cols],
                lambda i: b_one.at[i // 2, i % 2, x, :, cols],
            )
            send(7, k, b_two.at[:, 1 - zl, :, cols], b_three.at[:, :, cols], over_zl)
        if stage == "4":
            arrive(7, k)
            add_into(2, lambda i: b_three.at[i, :, cols], lambda i: b_two.at[i, zl, :, cols])
            send(8, k, b_three.at[1 - zh, :, cols], b_four.at[:, cols], over_zh)
        if stage == "5":
            arrive(8, k)
            f_ref[c, 1, y, :, cols] = (
                b_four[:, cols].astype(jnp.float32) + b_three[zh, :, cols].astype(jnp.float32)
            ).astype(jnp.bfloat16)
            own_rows = f_ref.at[c, 1, y, :, cols]
            send(9, k, own_rows, own_rows, over_y)
        if stage == "6":
            arrive(5, k)
            for half in range(2):
                at = pl.ds(half * q, q)
                f_ref[c, 0, half, :, cols] = (
                    a_three[at, cols].astype(jnp.float32) + a_four[at, cols].astype(jnp.float32)
                ).astype(jnp.bfloat16)
            arrive(9, k)
            both = f_ref.at[c, :, :, :, cols]
            send(10, k, both, both, over_c)
        if stage == "7":
            arrive(10, k)

    return step


BACKWARD_ORDER = (
    "begin",
    "st:0",
    "datt",
    "g1",
    "S0",
    "g2",
    "bld:1",
    "r1:0",
    "bld:0",
    "r1:1",
    "take:0",
    "r1:2",
    "home0",
    "st:1",
    "bld:2",
    "take:2",
    "bld:4",
    "r1:3",
    "r2a:0",
    "r2b:0",
    "r1:4",
    "r1:5",
    "take:1",
    "take:4",
    "bld:3",
    "take:3",
    "r2a:1",
    "r3a:0",
    "bld:5",
    "take:5",
    "at:1",
    "r2a:2",
    "r3a:1",
    "at:0",
    "r4a:0",
    "at:2",
    "r2a:3",
    "r3a:2",
    "pl",
    "r3a:3",
    "r4a:1",
    "r3:0",
    "r2b:3",
    "r4a:2",
    "r2b:4",
    "r2b:1",
    "r2a:4",
    "hE0",
    "st:2",
    "r2b:2",
    "ph",
    "r2a:5",
    "dw",
    "r4:0",
    "r4a:3",
    "r3a:4",
    "r2b:5",
    "r3:4",
    "ab:0",
    "ab:1",
    "r3a:5",
    "r3:3",
    "st:3",
    "r3:1",
    "r5:0",
    "r4:4",
    "r3:2",
    "r4a:4",
    "r3:5",
    "st:4",
    "hb:0",
    "da",
    "ha:0",
    "hb:1",
    "r6:0",
    "r4a:5",
    "stE",
    "r4:3",
    "r7:0",
    "ha:1",
    "r4:1",
    "r5:4",
    "r4:2",
    "r4:5",
    "r6:4",
    "r7:4",
    "wy",
    "hm:0",
    "r5:3",
    "hm:1",
    "r5:1",
    "r5:2",
    "r5:5",
    "wc",
    "r6:3",
    "r6:1",
    "hE:0",
    "r6:2",
    "r6:5",
    "wE",
    "r7:3",
    "r7:1",
    "r7:2",
    "r7:5",
    "hE:1",
)


def backward_kernel(
    parts,
    datt_ref,
    order_ref,
    out_my,
    stats_ref,
    vec_ref,
    att_hbm,
    dbranch_hbm,
    low_hbm,
    dsecond_hbm,
    act_hbm,
    dinner_hbm,
    sorted_hbm,
    prob_hbm,
    wsel_hbm,
    x_hbm,
    delta_hbm,
    out_home,
    grad_home,
    f_ref,
    w_all,
    stats_out,
    att_ref,
    dbranch_ref,
    low_ref,
    dsecond_ref,
    act_ref,
    dinner_ref,
    sorted_ref,
    prob_ref,
    wsel_ref,
    x_all,
    delta_ref,
    g_ref,
    datt_send,
    datt_in,
    gather,
    gathered,
    dsorted,
    scatter,
    dqkv,
    part_send,
    part_in,
    total,
    a_in,
    b_in,
    a_two,
    b_two,
    grad_my,
    dw,
    dw_y,
    dw_in,
    dw_all,
    stats_buf,
    stats_in,
    core_in,
    r_a_one,
    r_a_two,
    r_a_three,
    r_a_four,
    r_b_one,
    r_b_two,
    r_b_three,
    r_b_four,
    datt_ssem,
    datt_rsem,
    part_ssem,
    part_rsem,
    swap_ssem,
    swap_rsem,
    dw_ssem,
    dw_rsem,
    stats_ssem,
    stats_rsem,
    red_ssem,
    red_rsem,
    load_sem,
):
    zh, zl, x, y, c = coordinates()
    s = 4 * zh + 2 * zl + x
    j = 2 * zl + x
    p = 4 * c + j
    block, width = datt_ref.shape
    group = 8 * block
    scale = 0.125
    matched = c == zh
    datt_sems, part_sems = (datt_ssem, datt_rsem), (part_ssem, part_rsem)
    swap_sems, dw_sems, stats_sems = (swap_ssem, swap_rsem), (dw_ssem, dw_rsem), (stats_ssem, stats_rsem)

    def member(flip):
        fc, fz, fx = flip // 4, (flip // 2) % 2, flip % 2
        mc, mz, mx = bits(c, fc), bits(zl, fz), bits(x, fx)
        return device(zh, mz, mx, y, mc), mc, 2 * mz + mx

    peers = [member(flip)[0] for flip in range(1, 8)]
    sibling, over_x, over_z = peers[3], peers[0], peers[1]
    swap_peer = device(1 - zh, zl, x, y, 1 - c)
    over_y = device(zh, zl, x, 1 - y, c)
    across = [device(1 - zh, bits(zl, f // 2), bits(x, f % 2), y, c) for f in range(4)]
    loads = [
        pltpu.make_async_copy(src, dst, load_sem.at[i])
        for i, (src, dst) in enumerate(
            (
                (att_hbm, att_ref),
                (dbranch_hbm, dbranch_ref),
                (low_hbm, low_ref),
                (dsecond_hbm, dsecond_ref),
                (act_hbm, act_ref),
                (dinner_hbm, dinner_ref),
                (sorted_hbm, sorted_ref),
                (prob_hbm, prob_ref),
                (wsel_hbm, wsel_ref),
                (x_hbm, x_all),
                (delta_hbm, delta_ref),
            )
        )
    ]
    for copy in loads:
        copy.start()
    greet(peers + [swap_peer, over_y] + across)

    def home_copy(src, dst, index, start):
        away = remote(src, dst, swap_sems, index, swap_peer)
        here = pltpu.make_async_copy(src, dst, swap_rsem.at[3 + index])

        @pl.when(matched)
        def _():
            here.start() if start else here.wait()

        @pl.when(jnp.logical_not(matched))
        def _():
            away.start() if start else away.wait()

    def tile(mc, mj):
        first = datt_ref[:, pl.ds(pl.multiple_of(mj * 128, 128), 128)]
        other = datt_ref[:, pl.ds(pl.multiple_of((4 + mj // 2) * 128, 128), 128)]
        return join(
            select_head(other.astype(jnp.float32), mj % 2, 0), select_head(first.astype(jnp.float32), mc, 1)
        ).astype(jnp.bfloat16)

    datt_copies = []

    def datt_out():
        for flip in (3, 7, 1, 5, 2, 6, 4):
            peer, mc, mj = member(flip)
            datt_send[flip] = tile(mc, mj)
            copy = remote(datt_send.at[flip], datt_in.at[p], datt_sems, flip - 1, peer)
            copy.start()
            datt_copies.append(copy)
        datt_in[p] = tile(c, j)

    stats_peers = (sibling, over_x, over_z, across[0], over_y)
    stats_copies = [
        remote(stats_buf.at[k], stats_in.at[k], stats_sems, k, peer) for k, peer in enumerate(stats_peers)
    ]

    def stats_step(k):
        if k == 0:
            stats_buf[0] = stats_ref[...]
        else:
            stats_copies[k - 1].wait()
            stats_buf[k] = stats_buf[k - 1] + stats_in[k - 1]
        if k < len(stats_peers):
            stats_copies[k].start()
        else:
            stats_out[...] = stats_buf[k]

    share = width // 8
    q = g_ref.shape[3] // 8
    top = 4 * q

    def outer_grads():
        def one(d, carry):
            columns = pl.ds(pl.multiple_of(d * 4 * share, 128), 4 * share)
            g_ref[d // 4, (d // 2) % 2, d % 2, top : top + 4 * share, :] = dot(
                act_ref[:, columns], dsecond_ref[...], 0, 0
            ).astype(jnp.bfloat16)
            return carry

        lax.fori_loop(0, 8, one, 0)

    def inner_grads():
        def one(i, carry):
            z, n = i // 4, i % 4
            rows = pl.ds(pl.multiple_of(z * 4 * share, 128), 4 * share)
            columns = pl.ds(pl.multiple_of(n * width, 128), width)
            grads = dot(low_ref[:, rows], dinner_ref[:, columns], 0, 0).astype(jnp.bfloat16)
            for k in range(4):
                at = pl.ds(pl.multiple_of(n * share, 16), share)
                g_ref[z, k // 2, k % 2, at, :] = grads[share * k : share * (k + 1)]
            return carry

        lax.fori_loop(0, 8, one, 0)

    def grads_first():
        for copy in loads[:6]:
            copy.wait()
        vectors = vec_ref[...].astype(jnp.bfloat16)
        for z in range(2):
            columns = slice(4 * share * z, 4 * share * (z + 1))
            grads = dot(att_ref[:, columns], dbranch_ref[...], 0, 0).astype(jnp.bfloat16)
            for k in range(4):
                rows = grads[share * k : share * (k + 1)]
                g_ref[z, k // 2, k % 2, 4 * share : 4 * share + share // 2, :] = rows[: share // 2]
                g_ref[z, k // 2, k % 2, 4 * share + share // 2 : top, :] = jnp.zeros_like(vectors)
                g_ref[z, k // 2, k % 2, top + 4 * share : top + 4 * share + share // 2, :] = rows[share // 2 :]
                g_ref[z, k // 2, k % 2, top + 4 * share + share // 2 :, :] = vectors
        pl.when(c == 0)(outer_grads)
        pl.when(c == 1)(inner_grads)

    def grads_second():
        pl.when(c == 0)(inner_grads)
        pl.when(c == 1)(outer_grads)

    reduction = reduce_steps(
        parts,
        g_ref,
        f_ref,
        (core_in, r_a_one, r_a_two, r_a_three, r_a_four, r_b_one, r_b_two, r_b_three, r_b_four),
        (red_ssem, red_rsem),
    )

    half = 1024 * c
    step = gather.shape[1]
    chunks = group * 3 // 2 // step

    def build(k):
        head, start = (0, k * step) if k * step < group else (1, half + k * step - group)
        build_gather(order_ref, head, start, step, gather.at[k % 2])

    arrivals = []

    def take(k):
        if not arrivals:
            for copy in datt_copies:
                copy.wait()
            arrivals.append(True)
        gathered[k * step : (k + 1) * step, :] = dot(
            gather[k % 2], datt_in[...].reshape(group, 128)
        ).astype(jnp.bfloat16)

    def attend_back(first_lanes):
        def one(i, carry):
            at = pl.ds(pl.multiple_of(i * 128, 128), 128)
            tile_zero, tile_one = sorted_ref[at, 0:128], sorted_ref[at, 128:256]
            low_lanes = lanes((128, 128)) < 64
            query_lanes = low_lanes if first_lanes else jnp.logical_not(low_lanes)
            weights = prob_ref[at, :]
            taken = gathered[at, :]
            taken = jnp.where(query_lanes, jnp.zeros_like(taken), taken)
            weight_grads = dot(taken, tile_zero, 1, 1)
            inside = jnp.sum(weights * weight_grads, axis=1, keepdims=True)
            score_grads = weights * (weight_grads - inside)
            low_grads = score_grads.astype(jnp.bfloat16)
            query_grads = dot(low_grads, tile_one) * scale
            key_grads = dot(low_grads, tile_zero, 0, 0) * scale
            value_grads = dot(weights.astype(jnp.bfloat16), taken, 0, 0)
            dsorted[at, 0:128] = jnp.where(query_lanes, query_grads, value_grads).astype(jnp.bfloat16)
            dsorted[at, 128:256] = jnp.where(query_lanes, key_grads, 0.0).astype(jnp.bfloat16)
            return carry

        return one

    loaded = []

    def attend_some(i):
        if not loaded:
            for copy in loads[6:]:
                copy.wait()
            loaded.append(True)
        lax.fori_loop(8 * i, 8 * i + 8, attend_back(i < 2), 0, unroll=4)

    def place(position):
        token = lax.broadcasted_iota(jnp.int32, (128, 128), 0) + position * block
        for t in range(block // 128):
            for head, start, count, base in ((0, 0, group, 0), (1, half, group // 2, group)):
                for k in range(count // 128):
                    ids = order_ref[head : head + 1, pl.ds(pl.multiple_of(start + 128 * k, 128), 128)]
                    scatter[128 * t : 128 * (t + 1), base + 128 * k : base + 128 * (k + 1)] = hot(
                        ids == token + 128 * t
                    )
        at = pl.ds(pl.multiple_of(position * block, block), block)
        dqkv[at, 0:256] = dot(scatter[:, 0:group], dsorted[0:group, :]).astype(jnp.bfloat16)
        dqkv[at, 256:512] = dot(scatter[:, group:], dsorted[group:, :]).astype(jnp.bfloat16)
        return dot(dqkv[at, :], wsel_ref[...], 1, 1)

    def part_copy(k):
        return remote(part_send.at[k], part_in.at[k], part_sems, k, sibling)

    def parts_away():
        def one(k, carry):
            part_send[k] = place(4 * (1 - c) + k).astype(jnp.bfloat16)
            part_copy(k).start()
            return carry

        lax.fori_loop(0, 4, one, 0)

    def parts_here():
        def one(k, carry):
            part = place(4 * c + k)
            part_copy(k).wait()
            total[k // 2, k % 2] = (part + part_in[k].astype(jnp.float32)).astype(jnp.bfloat16)
            return carry

        lax.fori_loop(0, 4, one, 0)

    upper, lower = pl.ds(0, block // 2), pl.ds(block // 2, block // 2)
    pieces = [pl.ds(i * (width // 2), width // 2) for i in range(2)]
    a_copies = [
        remote(total.at[:, 1 - x, upper, cols], a_in.at[:, :, cols], part_sems, 4 + i, over_x)
        for i, cols in enumerate(pieces)
    ]
    b_copies = [
        remote(total.at[1 - zl, :, lower, cols], b_in.at[:, :, cols], part_sems, 6 + i, over_z)
        for i, cols in enumerate(pieces)
    ]
    a_next = [
        remote(a_in.at[1 - zl, :, cols], a_two.at[:, cols], part_sems, 8 + i, over_z)
        for i, cols in enumerate(pieces)
    ]
    b_next = [
        remote(b_in.at[1 - x, :, cols], b_two.at[:, cols], part_sems, 10 + i, over_x)
        for i, cols in enumerate(pieces)
    ]

    def first_hops(i):
        a_copies[i].start()
        b_copies[i].start()

    def second_hop_a(i):
        cols = pieces[i]
        a_copies[i].wait()
        add_into(2, lambda k: a_in.at[k, :, cols], lambda k: total.at[k, x, upper, cols])
        a_next[i].start()

    def second_hop_b(i):
        cols = pieces[i]
        b_copies[i].wait()
        add_into(2, lambda k: b_in.at[k, :, cols], lambda k: total.at[zl, k, lower, cols])
        b_next[i].start()

    def grad_home_start(i):
        cols = pieces[i]
        a_next[i].wait()
        b_next[i].wait()
        for start, first, second, index in ((0, a_two, a_in, zl), (block // 2, b_two, b_in, x)):
            at = pl.ds(start, block // 2)
            grad_my[at, cols] = (
                delta_ref[at, cols]
                + first[:, cols].astype(jnp.float32)
                + second[index, :, cols].astype(jnp.float32)
            ).astype(jnp.bfloat16)
        home_copy(grad_my.at[:, cols], grad_home.at[:, cols], 1 + i, True)

    def grad_home_end(i):
        cols = pieces[i]
        home_copy(grad_my.at[:, cols], grad_home.at[:, cols], 1 + i, False)

    over_y_copy = remote(dw_y.at[1 - y], dw_in, dw_sems, 0, over_y)

    def projections():
        for k in range(width // 128):
            dw[128 * k : 128 * (k + 1), :] = dot(
                x_all[:, 128 * k : 128 * (k + 1)], dqkv[...], 0, 0
            ).astype(jnp.bfloat16)
        bias_row = jnp.broadcast_to(
            jnp.sum(dqkv[...].astype(jnp.float32), axis=0, keepdims=True), (16, 512)
        ).astype(jnp.bfloat16)
        for d in range(8):
            for h in range(2):
                dw_y[h, d, 0:share, :] = dw[share * d : share * (d + 1), 256 * h : 256 * (h + 1)]
                dw_y[h, d, share : share + 16, :] = bias_row[:, 256 * h : 256 * (h + 1)]
        over_y_copy.start()

    targets = across + [over_x, over_z, peers[2]]
    flips = [(1, f // 2, f % 2) for f in range(4)] + [(0, 0, 1), (0, 1, 0), (0, 1, 1)]
    dw_copies = []
    for i, (peer, (fh, fz, fx)) in enumerate(zip(targets, flips)):
        d = 4 * bits(zh, fh) + 2 * bits(zl, fz) + bits(x, fx)
        dw_copies.append(remote(dw_y.at[y, d], dw_all.at[s], dw_sems, 1 + i, peer))
    w_over_y = remote(w_all.at[y, c], w_all.at[y, c], dw_sems, 8, over_y)
    w_over_c = remote(w_all.at[:, c], w_all.at[:, c], dw_sems, 9, sibling)

    def dw_exchange():
        over_y_copy.wait()
        add_into(8, lambda i: dw_y.at[y, i], lambda i: dw_in.at[i])
        for copy in dw_copies:
            copy.start()
        dw_all[s] = dw_y[y, s]

    def dw_sum():
        for copy in dw_copies:
            copy.wait()
        for k in range(4):
            w_all[y, c, k] = (dw_all[k].astype(jnp.float32) + dw_all[4 + k].astype(jnp.float32)).astype(
                jnp.bfloat16
            )
        w_over_y.start()

    def dw_core():
        w_over_y.wait()
        w_over_c.start()

    def start_reduction():
        for k in range(parts):
            reduction("0", k)

    single = {
        "begin": lambda: None,
        "datt": datt_out,
        "home0": lambda: home_copy(out_my, out_home, 0, True),
        "hE0": lambda: home_copy(out_my, out_home, 0, False),
        "g1": grads_first,
        "g2": grads_second,
        "S0": start_reduction,
        "pl": parts_away,
        "ph": parts_here,
        "dw": projections,
        "da": dw_exchange,
        "wy": dw_sum,
        "wc": dw_core,
        "wE": w_over_c.wait,
        "stE": lambda: stats_step(5),
    }
    indexed = {
        "bld": build,
        "take": take,
        "at": attend_some,
        "ab": first_hops,
        "ha": second_hop_a,
        "hb": second_hop_b,
        "hm": grad_home_start,
        "hE": grad_home_end,
        "st": stats_step,
    }
    for name in BACKWARD_ORDER:
        kind, _, index = name.partition(":")
        if kind in single:
            single[kind]()
        elif kind in indexed:
            indexed[kind](int(index))
        else:
            reduction(kind[1:], int(index))


def backward_attention(
    datt,
    order,
    output,
    stats,
    vectors,
    att,
    dbranch,
    low_first,
    dsecond,
    act,
    dinner,
    sorted_rows,
    prob,
    wsel,
    x_all,
    delta,
    parts,
):
    block, width = datt.shape
    inner_width = act.shape[1]
    group = 8 * block
    rows = group * 3 // 2
    q = (9 * width // 8 + 32) // 8
    share = width // 8 + 16
    low, full = jnp.bfloat16, jnp.float32
    vmem = pl.BlockSpec(memory_space=pltpu.VMEM)
    hbm = pl.BlockSpec(memory_space=pl.ANY)
    dma = pltpu.SemaphoreType.DMA
    shape = jax.ShapeDtypeStruct
    return pl.pallas_call(
        functools.partial(backward_kernel, parts),
        out_shape=[
            shape((block, width), low),
            shape((block, width), low),
            shape((2, 2, 2, q, width), low),
            shape((2, 2, 4, share, 256), low),
            shape(stats.shape, full),
        ],
        in_specs=[vmem] * 5 + [hbm] * 11,
        out_specs=[vmem] * 5,
        scratch_shapes=[
            pltpu.VMEM((block, width), low),
            pltpu.VMEM((block, width), low),
            pltpu.VMEM((block, width), low),
            pltpu.VMEM((block, width), low),
            pltpu.VMEM((block, inner_width), low),
            pltpu.VMEM((block, inner_width), low),
            pltpu.VMEM((rows, 256), low),
            pltpu.VMEM((rows, 128), full),
            pltpu.VMEM((width, 512), low),
            pltpu.VMEM((group, width), low),
            pltpu.VMEM((block, width), full),
            pltpu.VMEM((2, 2, 2, 8 * q, width), low),
            pltpu.VMEM((8, block, 128), low),
            pltpu.VMEM((8, block, 128), low),
            pltpu.VMEM((2, 512, group), low),
            pltpu.VMEM((rows, 128), low),
            pltpu.VMEM((rows, 256), low),
            pltpu.VMEM((block, rows), low),
            pltpu.VMEM((group, 512), low),
            pltpu.VMEM((4, block, width), low),
            pltpu.VMEM((4, block, width), low),
            pltpu.VMEM((2, 2, block, width), low),
            pltpu.VMEM((2, block // 2, width), low),
            pltpu.VMEM((2, block // 2, width), low),
            pltpu.VMEM((block // 2, width), low),
            pltpu.VMEM((block // 2, width), low),
            pltpu.VMEM((block, width), low),
            pltpu.VMEM((width, 512), low),
            pltpu.VMEM((2, 8, share, 256), low),
            pltpu.VMEM((8, share, 256), low),
            pltpu.VMEM((8, share, 256), low),
            pltpu.VMEM((6,) + stats.shape, full),
            pltpu.VMEM((5,) + stats.shape, full),
            pltpu.VMEM((2, 2, 2, 4 * q, width), low),
            pltpu.VMEM((2, 2, 2 * q, width), low),
            pltpu.VMEM((2, 2 * q, width), low),
            pltpu.VMEM((2 * q, width), low),
            pltpu.VMEM((2 * q, width), low),
            pltpu.VMEM((2, 2, 2, q, width), low),
            pltpu.VMEM((2, 2, q, width), low),
            pltpu.VMEM((2, q, width), low),
            pltpu.VMEM((q, width), low),
            dma((7,)),
            dma((7,)),
            dma((12,)),
            dma((12,)),
            dma((6,)),
            dma((6,)),
            dma((10,)),
            dma((10,)),
            dma((5,)),
            dma((5,)),
            dma((11, parts)),
            dma((11, parts)),
            dma((11,)),
        ],
        compiler_params=pltpu.CompilerParams(
            collective_id=2, has_side_effects=True, vmem_limit_bytes=62 << 20
        ),
        name="backward_attention",
    )(
        datt,
        order,
        output,
        stats,
        vectors,
        att,
        dbranch,
        low_first,
        dsecond,
        act,
        dinner,
        sorted_rows,
        prob,
        wsel,
        x_all.reshape(group, width),
        delta,
    )


def finish_kernel(
    f_ref,
    w_ref,
    out_ref,
    grad_ref,
    stats_ref,
    output,
    grad_tokens,
    gq_out,
    gqb_out,
    gk_out,
    gv_out,
    gvb_out,
    go_out,
    gob_out,
    gfg_out,
    gfs_out,
    gi_out,
    gib_out,
    gu_out,
    gub_out,
    gsg_out,
    gss_out,
    stats_out,
    gq_ref,
    gv_ref,
    vec_ref,
    square,
):
    s = lax.axis_index("seq")
    output[0] = out_ref[...]
    grad_tokens[0] = grad_ref[...]
    for kind in range(2):
        square[0:16, :] = stats_ref[kind]
        stats_out[kind] = square[...].T[: stats_out.shape[1], : stats_out.shape[2]]
    share, width = gk_out.shape
    top = f_ref.shape[0] // 2
    full = jnp.float32
    for n in range(gi_out.shape[1] // width):
        gi_out[:, n * width : (n + 1) * width] = f_ref[n * share : (n + 1) * share, :].astype(full)
    gu_out[...] = f_ref[top : top + 4 * share, :].astype(full)
    part = share // 2
    go_out[0:part, :] = f_ref[4 * share : 4 * share + part, :].astype(full)
    go_out[part:, :] = f_ref[top + 4 * share : top + 4 * share + part, :].astype(full)
    vec_ref[...] = f_ref[top + 4 * share + part :, :].astype(full)
    for pair in range(4):
        at = slice(128 * pair, 128 * pair + 128)
        low, high = (w_ref[0, core, pair].astype(full) for core in range(2))
        gq_ref[:, at] = join(low[:, 0:128], half_roll(high[:, 0:128]))
        gk_out[:, at] = join(low[:, 128:256], half_roll(high[:, 128:256]))[:share]
        gv_ref[:, at] = join(half_roll(low[:, 0:128]), high[:, 0:128])
    for pair in range(2):
        at = slice(512 + 128 * pair, 640 + 128 * pair)
        low, high = (
            w_ref[1, 0, 2 * pair + i].astype(full) + w_ref[1, 1, 2 * pair + i].astype(full) for i in range(2)
        )
        gq_ref[:, at] = join(half_roll(low[:, 0:128]), high[:, 0:128])
        gk_out[:, at] = join(half_roll(low[:, 128:256]), high[:, 128:256])[:share]
        gv_ref[:, at] = join(low[:, 0:128], half_roll(high[:, 0:128]))
    gq_out[...] = gq_ref[:share, :]
    gv_out[...] = gv_ref[:share, :]

    def mine(rows):
        return pltpu.roll(rows, width - share * s, 1)[:, :share]

    short = mine(vec_ref[...])
    for row, ref in enumerate((gob_out, gfg_out, gfs_out, gub_out, gsg_out, gss_out)):
        ref[...] = short[row]
    gqb_out[...] = mine(gq_ref[share : share + 8, :])[0]
    gvb_out[...] = mine(gv_ref[share : share + 8, :])[0]
    row = vec_ref[pl.ds(6 + s // 2, 1), :]
    gib_out[...] = jnp.where(s % 2 == 1, row[:, 4 * share :], row[:, : 4 * share])[0]


def finish(reduced, w_all, output, grad, totals, head_count, inner_width):
    block, width = output.shape
    row_count = 8 * reduced.shape[3]
    share = width // 8
    low, full = jnp.bfloat16, jnp.float32
    vmem = pl.BlockSpec(memory_space=pltpu.VMEM)
    shape = jax.ShapeDtypeStruct
    square, vector = shape((share, width), full), shape((share,), full)
    out_shape = [
        shape((1, block, width), low),
        shape((1, block, width), low),
        square,
        vector,
        square,
        square,
        vector,
        square,
        vector,
        vector,
        vector,
        shape((share, inner_width), full),
        shape((inner_width // 8,), full),
        shape((inner_width // 8, width), full),
        vector,
        vector,
        vector,
        shape((2, 8, head_count), full),
    ]
    outs = pl.pallas_call(
        finish_kernel,
        out_shape=out_shape,
        in_specs=[vmem] * 5,
        out_specs=[vmem] * len(out_shape),
        scratch_shapes=[
            pltpu.VMEM((share + 16, width), full),
            pltpu.VMEM((share + 16, width), full),
            pltpu.VMEM((16, width), full),
            pltpu.VMEM((128, 128), full),
        ],
        compiler_params=pltpu.CompilerParams(vmem_limit_bytes=60 << 20),
        name="finish",
    )(reduced.reshape(row_count, width), w_all, output, grad, totals)
    return (*outs[:-1], outs[-1].transpose(0, 2, 1))


def body(
    tokens,
    segments,
    orders,
    owners,
    query_weight,
    query_bias,
    key_weight,
    value_weight,
    value_bias,
    out_weight,
    out_bias,
    first_gain,
    first_shift,
    inner_weight,
    inner_bias,
    outer_weight,
    outer_bias,
    second_gain,
    second_shift,
    cotangent,
):
    seq_count = lax.axis_size("seq")
    groups = lax.axis_size("rep")
    own_index = lax.axis_index("seq")
    row_count = tokens.shape[1]
    model_width = tokens.shape[2]
    order_table = orders[0]
    owner_table = owners[0]
    head_count, group_tokens = order_table.shape
    cluster_count = owner_table.shape[1]
    cluster = group_tokens // cluster_count
    head_dim = model_width // head_count
    per_owner = row_count // cluster
    score_scale = head_dim ** (-0.5)
    flat_tokens = tokens[0]
    local_index = jnp.arange(row_count, dtype=jnp.int32)
    factor = 1
    for candidate in range(1, seq_count + 1):
        if seq_count % candidate == 0 and candidate * row_count <= 2048:
            factor = candidate
    block_count = seq_count // factor
    block_width = factor * row_count
    order_blocks = order_table.reshape(head_count, block_count, block_width).transpose(1, 0, 2)
    owner_blocks = (
        jnp.repeat(owner_table, cluster, axis=1)
        .reshape(head_count, block_count, block_width)
        .transpose(1, 0, 2)
    )

    def find_target(total, block_item):
        order_block, owner_block = block_item
        local = order_block - own_index * row_count
        hits = local[:, :, None] == local_index[None, None, :]
        return (total + jnp.sum(jnp.where(hits, owner_block[:, :, None], 0), axis=1), None)

    target, unused = lax.scan(
        find_target, jnp.zeros((head_count, row_count), jnp.int32), (order_blocks, owner_blocks)
    )
    send_matrix = rank_matrix(target * row_count + local_index[None, :])
    mine = (owner_table == own_index).astype(jnp.int32)
    before = jnp.cumsum(mine, axis=1) - mine
    slot_hot = (mine[:, None, :] == 1) & (
        before[:, None, :] == jnp.arange(per_owner, dtype=jnp.int32)[None, :, None]
    )
    order_grid = order_table.reshape(head_count, cluster_count, cluster)
    owned_tokens = jnp.sum(
        jnp.where(slot_hot[:, :, :, None], order_grid[:, None, :, :], 0), axis=2
    ).reshape(head_count, row_count)
    arrive_matrix = rank_matrix(owned_tokens)
    w_three = jnp.concatenate([query_weight, key_weight, value_weight], axis=1)
    bias_three = jnp.concatenate(
        [
            query_bias.astype(jnp.float32),
            jnp.zeros((model_width,), jnp.float32),
            value_bias.astype(jnp.float32),
        ]
    )
    projected = (
        jnp.dot(flat_tokens, w_three, preferred_element_type=jnp.float32) + bias_three
    ).astype(jnp.bfloat16)
    token_rows = (
        projected.reshape(row_count, 3, head_count, head_dim)
        .transpose(2, 0, 1, 3)
        .reshape(head_count, row_count, 3 * head_dim)
    )
    segment_rows = jnp.broadcast_to(
        segments[0].astype(jnp.bfloat16)[None, :, None], (head_count, row_count, 1)
    )
    send_values = scatter_rows(token_rows, send_matrix, seq_count)
    send_segments = scatter_rows(segment_rows, send_matrix, seq_count)
    arrived, arrived_segments = (
        lax.all_to_all(send_values, "seq", split_axis=0, concat_axis=0, tiled=True),
        lax.all_to_all(send_segments, "seq", split_axis=0, concat_axis=0, tiled=True),
    )
    cluster_rows = collect_rows(arrived, arrive_matrix, 3 * head_dim).reshape(
        head_count * per_owner, cluster, 3, head_dim
    )
    cluster_segments = collect_rows(arrived_segments, arrive_matrix, 1).reshape(
        head_count * per_owner, cluster
    )
    queries = cluster_rows[:, :, 0]
    keys_in = cluster_rows[:, :, 1]
    values = cluster_rows[:, :, 2]
    attended, log_total, entropy, occupied = cluster_forward(
        queries, keys_in, values, cluster_segments, score_scale
    )
    per_head = jnp.stack(
        [
            jnp.sum(entropy.reshape(head_count, -1), axis=1),
            jnp.sum(occupied.reshape(head_count, -1), axis=1) / cluster,
        ]
    ) / (groups * row_count)
    column = (jnp.arange(seq_count, dtype=jnp.int32) == own_index).astype(jnp.float32)
    cluster_stats = lax.psum(per_head[:, :, None] * column, ("seq", "rep"))
    leaving = scatter_rows(
        attended.reshape(head_count, row_count, head_dim), arrive_matrix, seq_count
    )
    returned = lax.all_to_all(leaving, "seq", split_axis=0, concat_axis=0, tiled=True)
    attended_rows = (
        collect_rows(returned, send_matrix, head_dim)
        .transpose(1, 0, 2)
        .reshape(row_count, model_width)
    )
    branch = jnp.dot(
        attended_rows, out_weight, preferred_element_type=jnp.float32
    ) + out_bias.astype(jnp.float32)
    first_out, normed_one, root_one = norm_forward(
        flat_tokens.astype(jnp.float32) + branch, first_gain, first_shift
    )
    first_low = first_out.astype(jnp.bfloat16)
    inner_sum = jnp.dot(
        first_low, inner_weight, preferred_element_type=jnp.float32
    ) + inner_bias.astype(jnp.float32)
    activated, gelu_pull = jax.vjp(exact_gelu, inner_sum)
    activated_low = activated.astype(jnp.bfloat16)
    second = jnp.dot(
        activated_low, outer_weight, preferred_element_type=jnp.float32
    ) + outer_bias.astype(jnp.float32)
    result, normed_two, root_two = norm_forward(first_out + second, second_gain, second_shift)
    output = result.astype(jnp.bfloat16)[None]
    upstream = cotangent[0].astype(jnp.float32)
    gradient_second_gain = jnp.sum(upstream * normed_two, axis=0)
    gradient_second_shift = jnp.sum(upstream, axis=0)
    delta_two = norm_backward(upstream, normed_two, root_two, second_gain)
    delta_second = delta_two.astype(jnp.bfloat16)
    gradient_outer_bias = jnp.sum(delta_second.astype(jnp.float32), axis=0)
    gradient_outer_weight = jnp.einsum(
        "tf,td->fd", activated_low, delta_second, preferred_element_type=jnp.float32
    )
    delta_activated = jnp.einsum(
        "td,fd->tf", delta_second, outer_weight, preferred_element_type=jnp.float32
    )
    delta_inner = gelu_pull(delta_activated)[0].astype(jnp.bfloat16)
    gradient_inner_bias = jnp.sum(delta_inner.astype(jnp.float32), axis=0)
    gradient_inner_weight = jnp.einsum(
        "td,tf->df", first_low, delta_inner, preferred_element_type=jnp.float32
    )
    delta_first = delta_two + jnp.einsum(
        "tf,df->td", delta_inner, inner_weight, preferred_element_type=jnp.float32
    )
    gradient_first_gain = jnp.sum(delta_first * normed_one, axis=0)
    gradient_first_shift = jnp.sum(delta_first, axis=0)
    delta_one = norm_backward(delta_first, normed_one, root_one, first_gain)
    delta_branch = delta_one.astype(jnp.bfloat16)
    gradient_out_bias = jnp.sum(delta_branch.astype(jnp.float32), axis=0)
    gradient_out_weight = jnp.einsum(
        "td,te->de", attended_rows, delta_branch, preferred_element_type=jnp.float32
    )
    delta_attended = jnp.einsum(
        "te,de->td", delta_branch, out_weight, preferred_element_type=jnp.float32
    ).astype(jnp.bfloat16)
    delta_rows = delta_attended.reshape(row_count, head_count, head_dim).transpose(1, 0, 2)
    send_grads = scatter_rows(delta_rows, send_matrix, seq_count)
    grad_arrived = lax.all_to_all(send_grads, "seq", split_axis=0, concat_axis=0, tiled=True)
    kept_queries, kept_keys, kept_values, kept_segments = (
        queries,
        keys_in,
        values,
        cluster_segments,
    )
    grad_cluster = collect_rows(grad_arrived, arrive_matrix, head_dim).reshape(
        head_count * per_owner, cluster, head_dim
    )
    three_grads = cluster_backward(
        kept_queries, kept_keys, kept_values, kept_segments, log_total, grad_cluster, score_scale
    )
    leaving_grads = scatter_rows(
        three_grads.reshape(head_count, row_count, 3 * head_dim), arrive_matrix, seq_count
    )
    returned_grads = lax.all_to_all(leaving_grads, "seq", split_axis=0, concat_axis=0, tiled=True)
    delta_three = (
        collect_rows(returned_grads, send_matrix, 3 * head_dim)
        .reshape(head_count, row_count, 3, head_dim)
        .transpose(1, 2, 0, 3)
        .reshape(row_count, 3 * model_width)
    )
    bias_grads = jnp.sum(delta_three.astype(jnp.float32), axis=0)
    weight_grads = jnp.einsum(
        "td,te->de", flat_tokens, delta_three, preferred_element_type=jnp.float32
    )
    gradient_tokens = (
        delta_one
        + jnp.einsum("te,de->td", delta_three, w_three, preferred_element_type=jnp.float32)
    ).astype(jnp.bfloat16)[None]
    gradient_query_weight = weight_grads[:, :model_width]
    gradient_key_weight = weight_grads[:, model_width : 2 * model_width]
    gradient_value_weight = weight_grads[:, 2 * model_width :]
    gradient_query_bias = bias_grads[:model_width]
    gradient_value_bias = bias_grads[2 * model_width :]
    pieces = (
        lax.psum_scatter(gradient_query_weight, "seq", scatter_dimension=0, tiled=True),
        lax.psum_scatter(gradient_query_bias, "seq", scatter_dimension=0, tiled=True),
        lax.psum_scatter(gradient_key_weight, "seq", scatter_dimension=0, tiled=True),
        lax.psum_scatter(gradient_value_weight, "seq", scatter_dimension=0, tiled=True),
        lax.psum_scatter(gradient_value_bias, "seq", scatter_dimension=0, tiled=True),
        lax.psum_scatter(gradient_out_weight, "seq", scatter_dimension=0, tiled=True),
        lax.psum_scatter(gradient_out_bias, "seq", scatter_dimension=0, tiled=True),
        lax.psum_scatter(gradient_first_gain, "seq", scatter_dimension=0, tiled=True),
        lax.psum_scatter(gradient_first_shift, "seq", scatter_dimension=0, tiled=True),
        lax.psum_scatter(gradient_inner_weight, "seq", scatter_dimension=0, tiled=True),
        lax.psum_scatter(gradient_inner_bias, "seq", scatter_dimension=0, tiled=True),
        lax.psum_scatter(gradient_outer_weight, "seq", scatter_dimension=0, tiled=True),
        lax.psum_scatter(gradient_outer_bias, "seq", scatter_dimension=0, tiled=True),
        lax.psum_scatter(gradient_second_gain, "seq", scatter_dimension=0, tiled=True),
        lax.psum_scatter(gradient_second_shift, "seq", scatter_dimension=0, tiled=True),
    )
    summed = (
        lax.psum(pieces[0].astype(jnp.bfloat16), "rep").astype(jnp.float32),
        lax.psum(pieces[1].astype(jnp.bfloat16), "rep").astype(jnp.float32),
        lax.psum(pieces[2].astype(jnp.bfloat16), "rep").astype(jnp.float32),
        lax.psum(pieces[3].astype(jnp.bfloat16), "rep").astype(jnp.float32),
        lax.psum(pieces[4].astype(jnp.bfloat16), "rep").astype(jnp.float32),
        lax.psum(pieces[5].astype(jnp.bfloat16), "rep").astype(jnp.float32),
        lax.psum(pieces[6].astype(jnp.bfloat16), "rep").astype(jnp.float32),
        lax.psum(pieces[7].astype(jnp.bfloat16), "rep").astype(jnp.float32),
        lax.psum(pieces[8].astype(jnp.bfloat16), "rep").astype(jnp.float32),
        lax.psum(pieces[9].astype(jnp.bfloat16), "rep").astype(jnp.float32),
        lax.psum(pieces[10].astype(jnp.bfloat16), "rep").astype(jnp.float32),
        lax.psum(pieces[11].astype(jnp.bfloat16), "rep").astype(jnp.float32),
        lax.psum(pieces[12].astype(jnp.bfloat16), "rep").astype(jnp.float32),
        lax.psum(pieces[13].astype(jnp.bfloat16), "rep").astype(jnp.float32),
        lax.psum(pieces[14].astype(jnp.bfloat16), "rep").astype(jnp.float32),
    )
    return (output, gradient_tokens) + tuple(summed) + (cluster_stats,)


def square_body(
    tokens,
    segments,
    orders,
    owners,
    query_weight,
    query_bias,
    key_weight,
    value_weight,
    value_bias,
    out_weight,
    out_bias,
    first_gain,
    first_shift,
    inner_weight,
    inner_bias,
    outer_weight,
    outer_bias,
    second_gain,
    second_shift,
    cotangent,
):
    (
        wsel,
        order,
        stats,
        x_all,
        sorted_rows,
        prob,
        att,
        low_first,
        act,
        output,
        dsecond,
        dinner,
        delta,
        dbranch,
        vector_grads,
        datt,
    ) = forward_layer(
        tokens[0],
        cotangent[0],
        segments,
        orders.transpose(1, 0, 2),
        owners.transpose(1, 0, 2),
        (
            query_bias,
            value_bias,
            out_bias,
            first_gain,
            first_shift,
            outer_bias,
            second_gain,
            second_shift,
            inner_bias,
        ),
        (query_weight, key_weight, value_weight, out_weight, inner_weight, outer_weight),
    )
    output, grad, reduced, w_all, totals = backward_attention(
        datt,
        order,
        output,
        stats,
        vector_grads,
        att,
        dbranch,
        low_first,
        dsecond,
        act,
        dinner,
        sorted_rows,
        prob,
        wsel,
        x_all,
        delta,
        6,
    )
    return finish(reduced, w_all, output, grad, totals, orders.shape[1], inner_weight.shape[1])


def solution(mesh):
    square = mesh.shape["seq"] == 8 and mesh.shape["rep"] == 4
    placed = (
        P("rep", "seq", None),
        P("rep", "seq"),
        P("rep", None, None),
        P("rep", None, None),
        P(),
        P(),
        P(),
        P(),
        P(),
        P(),
        P(),
        P(),
        P(),
        P(),
        P(),
        P(),
        P(),
        P(),
        P(),
        P("rep", "seq", None),
    )
    return jax.shard_map(
        square_body if square else body,
        mesh=mesh,
        in_specs=placed,
        out_specs=(
            P("rep", "seq", None),
            P("rep", "seq", None),
            P("seq", None),
            P("seq"),
            P("seq", None),
            P("seq", None),
            P("seq"),
            P("seq", None),
            P("seq"),
            P("seq"),
            P("seq"),
            P("seq", None),
            P("seq"),
            P("seq", None),
            P("seq"),
            P("seq"),
            P("seq"),
            P(),
        ),
        check_vma=False,
    )
```

profile of v0, /device:TPU:0, one launch (start us, length us, event | category | flops | bytes accessed | tf_op | source)
XLA Modules:
  0.0 164.5 jit_solution(15125896817088912116)
XLA Ops:
  0.7 61.9 %forward_layer.1 = (bf16[768,512]{1,0:T(8,128)(2,1)}, s32[8,2048]{1,0:T(8,128)}, f32[2,16,128]{2,1,0:T(8,128)}, bf16[8,256,768]{2,1,0:T(8,128)(2,1)}, bf16[3072,...) custom-call(bf16[256,768]{1,0:T(8,128)(2,1)} %bitcast.9, ...), custom_call_target="tpu_custom_call" | custom-call | tf_op jit(solution)/shard_map/forward_layer/pallas_call | solution.py:786
  62.5 97.6 %backward_attention.1 = (bf16[256,768]{1,0:T(8,128)(2,1)}, bf16[256,768]{1,0:T(8,128)(2,1)}, bf16[2,2,2,112,768]{4,3,2,1,0:T(8,128)(2,1)}, bf16[2,2,4,112,256]{4,3,2,1,0:T(8,128)(2,1)}, f32[2,16,128]{2,1,0:T(8,128)}) custom-call(bf16[256,768]{1,0:T(8,128)(2,1)} %get-tuple-element.57.datt_ref, s32[8,2048]{1,0:T(8,128)} %get-tuple-element.58.order_ref, ...), custom_call_target="tpu_custom_call" | custom-call | tf_op jit(solution)/shard_map/backward_attention/pallas_call | solution.py:1527
  160.2 4.2 %finish.1 = (bf16[1,256,768]{2,1,0:T(8,128)(2,1)}, bf16[1,256,768]{2,1,0:T(8,128)(2,1)}, f32[96,768]{1,0:T(8,128)}, f32[96]{0:T(128)}, f32[96,768]{1,0:T(8,128)}...) custom-call(bf16[896,768]{1,0:T(8,128)(2,1)} %bitcast.8, ...), custom_call_target="tpu_custom_call" | custom-call | tf_op jit(solution)/shard_map/finish/pallas_call | solution.py:1721
where the time goes:
time: 165 us
  Pallas kernels  164 us (99%)
    pallas_call x1, Pallas kernels, backward_attention(): pl.pallas_call(functools.partial(backward_kernel, parts), out_shape=[shap...  97.6 us
    pallas_call x1, Pallas kernels, forward_layer(): pl.pallas_call(forward_kernel, out_shape=[jax.ShapeDtypeStruct(*one) for...  61.9 us
    pallas_call x1, Pallas kernels, finish(): pl.pallas_call(finish_kernel, out_shape=out_shape, in_specs=[vmem] * 5, o...  4.19 us

commit v1 on v0

--- a/solution.py
+++ b/solution.py
@@ -847,7 +847,7 @@
     lax.fori_loop(0, count, one, 0)
 
 
-def reduce_steps(parts, g_ref, f_ref, buffers, sems):
+def reduce_steps(parts, g_ref, f_ref, f_hbm, buffers, sems, out_sem):
     core_in, a_one, a_two, a_three, a_four, b_one, b_two, b_three, b_four = buffers
     zh, zl, x, y, c = coordinates()
     q = g_ref.shape[3] // 8
@@ -855,7 +855,7 @@
     over_c, over_y = device(zh, zl, x, y, 1 - c), device(zh, zl, x, 1 - y, c)
     over_x, over_zl = device(zh, zl, 1 - x, y, c), device(zh, 1 - zl, x, y, c)
     over_zh = device(1 - zh, zl, x, y, c)
-    flying = {}
+    flying, outward = {}, []
 
     def send(name, k, src, dst, peer):
         copy = remote(src, dst, (sems[0].at[name], sems[1].at[name]), k, peer)
@@ -935,114 +935,117 @@
             send(10, k, both, both, over_c)
         if stage == "7":
             arrive(10, k)
-
-    return step
+            copy = pltpu.make_async_copy(f_ref.at[:, :, :, :, cols], f_hbm.at[:, :, :, :, cols], out_sem.at[k])
+            copy.start()
+            outward.append(copy)
+
+    return step, outward
 
 
 BACKWARD_ORDER = (
     "begin",
-    "st:0",
+    "home0",
     "datt",
     "g1",
     "S0",
     "g2",
+    "bld:0",
+    "r1:0",
+    "st:0",
     "bld:1",
-    "r1:0",
-    "bld:0",
+    "take:0",
     "r1:1",
-    "take:0",
     "r1:2",
-    "home0",
-    "st:1",
+    "hE0",
     "bld:2",
     "take:2",
+    "r1:3",
+    "r1:4",
+    "take:1",
+    "r2b:0",
+    "r1:5",
+    "st:1",
+    "r2a:0",
     "bld:4",
-    "r1:3",
-    "r2a:0",
-    "r2b:0",
-    "r1:4",
-    "r1:5",
-    "take:1",
     "take:4",
     "bld:3",
+    "r2b:1",
+    "r2a:1",
     "take:3",
-    "r2a:1",
-    "r3a:0",
     "bld:5",
     "take:5",
     "at:1",
+    "at:0",
     "r2a:2",
-    "r3a:1",
-    "at:0",
-    "r4a:0",
+    "r2b:2",
     "at:2",
     "r2a:3",
+    "r3a:0",
+    "pl",
     "r3a:2",
-    "pl",
+    "r2b:4",
+    "r2a:4",
+    "r3a:1",
+    "r2b:3",
     "r3a:3",
-    "r4a:1",
+    "r4a:0",
     "r3:0",
-    "r2b:3",
+    "ph",
     "r4a:2",
-    "r2b:4",
-    "r2b:1",
-    "r2a:4",
-    "hE0",
     "st:2",
-    "r2b:2",
-    "ph",
-    "r2a:5",
-    "dw",
-    "r4:0",
-    "r4a:3",
     "r3a:4",
     "r2b:5",
+    "ab:0",
+    "dw",
+    "r4a:3",
+    "st:3",
+    "r4:0",
+    "r3:2",
+    "r3:1",
+    "r2a:5",
+    "ab:1",
+    "r4a:4",
+    "r4a:1",
+    "st:4",
     "r3:4",
-    "ab:0",
-    "ab:1",
+    "hb:0",
+    "r5:0",
+    "r4:2",
+    "r3:3",
+    "r4:1",
+    "r3:5",
     "r3a:5",
-    "r3:3",
-    "st:3",
-    "r3:1",
-    "r5:0",
-    "r4:4",
-    "r3:2",
-    "r4a:4",
-    "r3:5",
-    "st:4",
-    "hb:0",
     "da",
     "ha:0",
     "hb:1",
+    "r4:4",
+    "r5:2",
+    "stE",
     "r6:0",
+    "r4:3",
+    "ha:1",
+    "r5:1",
+    "r6:2",
+    "r7:0",
+    "r4:5",
+    "r6:1",
+    "r7:2",
     "r4a:5",
-    "stE",
-    "r4:3",
-    "r7:0",
-    "ha:1",
-    "r4:1",
-    "r5:4",
-    "r4:2",
-    "r4:5",
-    "r6:4",
-    "r7:4",
+    "r7:1",
     "wy",
     "hm:0",
+    "r5:4",
     "r5:3",
     "hm:1",
-    "r5:1",
-    "r5:2",
     "r5:5",
     "wc",
+    "r6:4",
     "r6:3",
-    "r6:1",
     "hE:0",
-    "r6:2",
     "r6:5",
     "wE",
+    "r7:4",
     "r7:3",
-    "r7:1",
-    "r7:2",
     "r7:5",
     "hE:1",
 )
@@ -1050,11 +1053,11 @@
 
 def backward_kernel(
     parts,
-    datt_ref,
-    order_ref,
+    datt_hbm,
+    order_hbm,
     out_my,
-    stats_ref,
-    vec_ref,
+    stats_hbm,
+    vec_hbm,
     att_hbm,
     dbranch_hbm,
     low_hbm,
@@ -1068,20 +1071,26 @@
     delta_hbm,
     out_home,
     grad_home,
-    f_ref,
-    w_all,
+    f_hbm,
+    w_hbm,
     stats_out,
+    datt_ref,
     att_ref,
     dbranch_ref,
+    vec_ref,
     low_ref,
     dsecond_ref,
     act_ref,
     dinner_ref,
+    order_ref,
+    stats_ref,
     sorted_ref,
     prob_ref,
     wsel_ref,
     x_all,
     delta_ref,
+    f_ref,
+    w_all,
     g_ref,
     datt_send,
     datt_in,
@@ -1126,6 +1135,7 @@
     red_ssem,
     red_rsem,
     load_sem,
+    out_sem,
 ):
     zh, zl, x, y, c = coordinates()
     s = 4 * zh + 2 * zl + x
@@ -1148,16 +1158,24 @@
     swap_peer = device(1 - zh, zl, x, y, 1 - c)
     over_y = device(zh, zl, x, 1 - y, c)
     across = [device(1 - zh, bits(zl, f // 2), bits(x, f % 2), y, c) for f in range(4)]
+    everyone = peers + [swap_peer, over_y] + across
+    barrier = pltpu.get_barrier_semaphore()
+    for peer in everyone:
+        pl.semaphore_signal(barrier, inc=1, device_id=peer, device_id_type=MESH)
     loads = [
         pltpu.make_async_copy(src, dst, load_sem.at[i])
         for i, (src, dst) in enumerate(
             (
+                (datt_hbm, datt_ref),
                 (att_hbm, att_ref),
                 (dbranch_hbm, dbranch_ref),
+                (vec_hbm, vec_ref),
                 (low_hbm, low_ref),
                 (dsecond_hbm, dsecond_ref),
                 (act_hbm, act_ref),
                 (dinner_hbm, dinner_ref),
+                (order_hbm, order_ref),
+                (stats_hbm, stats_ref),
                 (sorted_hbm, sorted_ref),
                 (prob_hbm, prob_ref),
                 (wsel_hbm, wsel_ref),
@@ -1168,7 +1186,6 @@
     ]
     for copy in loads:
         copy.start()
-    greet(peers + [swap_peer, over_y] + across)
 
     def home_copy(src, dst, index, start):
         away = remote(src, dst, swap_sems, index, swap_peer)
@@ -1191,14 +1208,17 @@
 
     datt_copies = []
 
+    def datt_tiles():
+        loads[0].wait()
+        for flip in range(1, 8):
+            peer, mc, mj = member(flip)
+            datt_send[flip] = tile(mc, mj)
+            datt_copies.append(remote(datt_send.at[flip], datt_in.at[p], datt_sems, flip - 1, peer))
+        datt_in[p] = tile(c, j)
+
     def datt_out():
         for flip in (3, 7, 1, 5, 2, 6, 4):
-            peer, mc, mj = member(flip)
-            datt_send[flip] = tile(mc, mj)
-            copy = remote(datt_send.at[flip], datt_in.at[p], datt_sems, flip - 1, peer)
-            copy.start()
-            datt_copies.append(copy)
-        datt_in[p] = tile(c, j)
+            datt_copies[flip - 1].start()
 
     stats_peers = (sibling, over_x, over_z, across[0], over_y)
     stats_copies = [
@@ -1207,6 +1227,7 @@
 
     def stats_step(k):
         if k == 0:
+            loads[9].wait()
             stats_buf[0] = stats_ref[...]
         else:
             stats_copies[k - 1].wait()
@@ -1214,7 +1235,9 @@
         if k < len(stats_peers):
             stats_copies[k].start()
         else:
-            stats_out[...] = stats_buf[k]
+            copy = pltpu.make_async_copy(stats_buf.at[k], stats_out, out_sem.at[parts])
+            copy.start()
+            outward.append(copy)
 
     share = width // 8
     q = g_ref.shape[3] // 8
@@ -1243,8 +1266,8 @@
 
         lax.fori_loop(0, 8, one, 0)
 
-    def grads_first():
-        for copy in loads[:6]:
+    def out_grads():
+        for copy in loads[1:4]:
             copy.wait()
         vectors = vec_ref[...].astype(jnp.bfloat16)
         for z in range(2):
@@ -1256,6 +1279,10 @@
                 g_ref[z, k // 2, k % 2, 4 * share + share // 2 : top, :] = jnp.zeros_like(vectors)
                 g_ref[z, k // 2, k % 2, top + 4 * share : top + 4 * share + share // 2, :] = rows[share // 2 :]
                 g_ref[z, k // 2, k % 2, top + 4 * share + share // 2 :, :] = vectors
+
+    def grads_first():
+        for copy in loads[4:9]:
+            copy.wait()
         pl.when(c == 0)(outer_grads)
         pl.when(c == 1)(inner_grads)
 
@@ -1263,12 +1290,14 @@
         pl.when(c == 0)(inner_grads)
         pl.when(c == 1)(outer_grads)
 
-    reduction = reduce_steps(
+    reduction, outward = reduce_steps(
         parts,
         g_ref,
         f_ref,
+        f_hbm,
         (core_in, r_a_one, r_a_two, r_a_three, r_a_four, r_b_one, r_b_two, r_b_three, r_b_four),
         (red_ssem, red_rsem),
+        out_sem,
     )
 
     half = 1024 * c
@@ -1316,7 +1345,7 @@
 
     def attend_some(i):
         if not loaded:
-            for copy in loads[6:]:
+            for copy in loads[10:]:
                 copy.wait()
             loaded.append(True)
         lax.fori_loop(8 * i, 8 * i + 8, attend_back(i < 2), 0, unroll=4)
@@ -1452,12 +1481,23 @@
         w_over_y.wait()
         w_over_c.start()
 
+    def dw_end():
+        w_over_c.wait()
+        copy = pltpu.make_async_copy(w_all, w_hbm, out_sem.at[parts + 1])
+        copy.start()
+        outward.append(copy)
+
+    def begin():
+        datt_tiles()
+        out_grads()
+        pl.semaphore_wait(barrier, len(everyone))
+
     def start_reduction():
         for k in range(parts):
             reduction("0", k)
 
     single = {
-        "begin": lambda: None,
+        "begin": begin,
         "datt": datt_out,
         "home0": lambda: home_copy(out_my, out_home, 0, True),
         "hE0": lambda: home_copy(out_my, out_home, 0, False),
@@ -1470,7 +1510,7 @@
         "da": dw_exchange,
         "wy": dw_sum,
         "wc": dw_core,
-        "wE": w_over_c.wait,
+        "wE": dw_end,
         "stE": lambda: stats_step(5),
     }
     indexed = {
@@ -1492,6 +1532,8 @@
             indexed[kind](int(index))
         else:
             reduction(kind[1:], int(index))
+    for copy in outward:
+        copy.wait()
 
 
 def backward_attention(
@@ -1533,20 +1575,26 @@
             shape((2, 2, 4, share, 256), low),
             shape(stats.shape, full),
         ],
-        in_specs=[vmem] * 5 + [hbm] * 11,
-        out_specs=[vmem] * 5,
+        in_specs=[hbm] * 16,
+        out_specs=[hbm] * 5,
         scratch_shapes=[
             pltpu.VMEM((block, width), low),
             pltpu.VMEM((block, width), low),
             pltpu.VMEM((block, width), low),
+            pltpu.VMEM(vectors.shape, full),
+            pltpu.VMEM((block, width), low),
             pltpu.VMEM((block, width), low),
             pltpu.VMEM((block, inner_width), low),
             pltpu.VMEM((block, inner_width), low),
+            pltpu.VMEM(order.shape, order.dtype),
+            pltpu.VMEM(stats.shape, full),
             pltpu.VMEM((rows, 256), low),
             pltpu.VMEM((rows, 128), full),
             pltpu.VMEM((width, 512), low),
             pltpu.VMEM((group, width), low),
             pltpu.VMEM((block, width), full),
+            pltpu.VMEM((2, 2, 2, q, width), low),
+            pltpu.VMEM((2, 2, 4, share, 256), low),
             pltpu.VMEM((2, 2, 2, 8 * q, width), low),
             pltpu.VMEM((8, block, 128), low),
             pltpu.VMEM((8, block, 128), low),
@@ -1590,7 +1638,8 @@
             dma((5,)),
             dma((11, parts)),
             dma((11, parts)),
-            dma((11,)),
+            dma((15,)),
+            dma((parts + 2,)),
         ],
         compiler_params=pltpu.CompilerParams(
             collective_id=2, has_side_effects=True, vmem_limit_bytes=62 << 20

time: 165 us -> 162 us (0.982); the launches traced: 165 us -> 160 us
  Pallas kernels: 164 us -> 159 us
    pallas_call x1, Pallas kernels: 97.6 us -> 92.7 us  [backward_attention(): pl.pallas_call(functools.partial(backward_kernel, parts), out_shape=[shap...]
where the time goes in v1:
time: 162 us; the launch traced here: 160 us
  Pallas kernels  159 us (98%)
    pallas_call x1, Pallas kernels, backward_attention(): pl.pallas_call(functools.partial(backward_kernel, parts), out_shape=[shap...  92.7 us
    pallas_call x1, Pallas kernels, forward_layer(): pl.pallas_call(forward_kernel, out_shape=[jax.ShapeDtypeStruct(*one) for...  61.9 us
    pallas_call x1, Pallas kernels, finish(): pl.pallas_call(finish_kernel, out_shape=out_shape, in_specs=[vmem] * 5, o...  4.19 us

profile of v1, /device:TPU:0, one launch (start us, length us, event | category | flops | bytes accessed | tf_op | source)
XLA Modules:
  0.0 159.6 jit_solution(17255936280690054)
XLA Ops:
  0.7 61.9 %forward_layer.1 = (bf16[768,512]{1,0:T(8,128)(2,1)}, s32[8,2048]{1,0:T(8,128)}, f32[2,16,128]{2,1,0:T(8,128)}, bf16[8,256,768]{2,1,0:T(8,128)(2,1)}, bf16[3072,...) custom-call(bf16[256,768]{1,0:T(8,128)(2,1)} %bitcast.9, ...), custom_call_target="tpu_custom_call" | custom-call | tf_op jit(solution)/shard_map/forward_layer/pallas_call | solution.py:786
  62.5 92.7 %backward_attention.1 = (bf16[256,768]{1,0:T(8,128)(2,1)}, bf16[256,768]{1,0:T(8,128)(2,1)}, bf16[2,2,2,112,768]{4,3,2,1,0:T(8,128)(2,1)}, bf16[2,2,4,112,256]{4,3,2,1,0:T(8,128)(2,1)}, f32[2,16,128]{2,1,0:T(8,128)}) custom-call(bf16[256,768]{1,0:T(8,128)(2,1)} %get-tuple-element.57.datt_hbm, s32[8,2048]{1,0:T(8,128)} %get-tuple-element.58.order_hbm, ...), custom_call_target="tpu_custom_call" | custom-call | tf_op jit(solution)/shard_map/backward_attention/pallas_call | solution.py:1569
  155.3 4.2 %finish.1 = (bf16[1,256,768]{2,1,0:T(8,128)(2,1)}, bf16[1,256,768]{2,1,0:T(8,128)(2,1)}, f32[96,768]{1,0:T(8,128)}, f32[96]{0:T(128)}, f32[96,768]{1,0:T(8,128)}...) custom-call(bf16[896,768]{1,0:T(8,128)(2,1)} %bitcast.8, ...), custom_call_target="tpu_custom_call" | custom-call | tf_op jit(solution)/shard_map/finish/pallas_call | solution.py:1770

commit v2 on v1

--- a/solution.py
+++ b/solution.py
@@ -352,9 +352,9 @@
         for i, src in enumerate((wq_hbm, wk_hbm, wv_hbm))
         for slot, index in enumerate((j, 4 + j // 2))
     ]
+    greet(peers + [swap_peer])
     for copy in slabs:
         copy.start()
-    greet(peers + [swap_peer])
     width_inner = inner_w.shape[1]
     dense_tile = 2 * width
     parts = [slice(dense_tile * t, dense_tile * (t + 1)) for t in range(width_inner // dense_tile)]

time: 162 us -> 161 us (level)
  no operation moved by 1% of the time
where the time goes in v2:
time: 161 us; the launch traced here: 159 us
  Pallas kernels  158 us (98%)
    pallas_call x1, Pallas kernels, backward_attention(): pl.pallas_call(functools.partial(backward_kernel, parts), out_shape=[shap...  92.8 us
    pallas_call x1, Pallas kernels, forward_layer(): pl.pallas_call(forward_kernel, out_shape=[jax.ShapeDtypeStruct(*one) for...  61.5 us
    pallas_call x1, Pallas kernels, finish(): pl.pallas_call(finish_kernel, out_shape=out_shape, in_specs=[vmem] * 5, o...  4.19 us

profile of v2, /device:TPU:0, one launch (start us, length us, event | category | flops | bytes accessed | tf_op | source)
XLA Modules:
  0.0 159.3 jit_solution(13150804474188370269)
XLA Ops:
  0.7 61.5 %forward_layer.1 = (bf16[768,512]{1,0:T(8,128)(2,1)}, s32[8,2048]{1,0:T(8,128)}, f32[2,16,128]{2,1,0:T(8,128)}, bf16[8,256,768]{2,1,0:T(8,128)(2,1)}, bf16[3072,...) custom-call(bf16[256,768]{1,0:T(8,128)(2,1)} %bitcast.9, ...), custom_call_target="tpu_custom_call" | custom-call | tf_op jit(solution)/shard_map/forward_layer/pallas_call | solution.py:786
  62.2 92.8 %backward_attention.1 = (bf16[256,768]{1,0:T(8,128)(2,1)}, bf16[256,768]{1,0:T(8,128)(2,1)}, bf16[2,2,2,112,768]{4,3,2,1,0:T(8,128)(2,1)}, bf16[2,2,4,112,256]{4,3,2,1,0:T(8,128)(2,1)}, f32[2,16,128]{2,1,0:T(8,128)}) custom-call(bf16[256,768]{1,0:T(8,128)(2,1)} %get-tuple-element.57.datt_hbm, s32[8,2048]{1,0:T(8,128)} %get-tuple-element.58.order_hbm, ...), custom_call_target="tpu_custom_call" | custom-call | tf_op jit(solution)/shard_map/backward_attention/pallas_call | solution.py:1569
  154.9 4.2 %finish.1 = (bf16[1,256,768]{2,1,0:T(8,128)(2,1)}, bf16[1,256,768]{2,1,0:T(8,128)(2,1)}, f32[96,768]{1,0:T(8,128)}, f32[96]{0:T(128)}, f32[96,768]{1,0:T(8,128)}...) custom-call(bf16[896,768]{1,0:T(8,128)(2,1)} %bitcast.8, ...), custom_call_target="tpu_custom_call" | custom-call | tf_op jit(solution)/shard_map/finish/pallas_call | solution.py:1770
